TPU v7x, 32 devices: a whole 2x2x4 slice. The times are simulated.
32 devices in a mesh: sta: 8 (over z, y), seg: 4 (over x, core).
Axes of the slice: x: 2, y: 2, z: 4, core: 2. Of those that a mesh axis runs over, the one named last changes fastest.
Arguments:
- records: bfloat16 [128, 8192], P('sta', 'seg'), may hold values from -300 to 300, as said below
- owners: int32 [64, 4], P('sta'), may hold values from 0 to 7, all different within a row; in each aligned block of 8 rows (0 to 7, 8 to 15, ...) at most 8 rows name the same one
Outputs:
- whitened: bfloat16 [128, 8192], P('sta', 'seg')
- correlations: bfloat16 [128, 128, 512], P('seg', 'sta')
Inputs may be any that keep to these rules, and one draw needn't show every extreme that they name: Each row names 4 different owners; among the 8 blocks of one index of sta no owner is named more than 8 times, some owner is named exactly 8 times, and every owner is named by some block. Real-valued records.
All inputs are finite; a program needn't handle non-finite values.
Results may differ from a plain program's by a relative error of at most 0.017.
Values may be sent and summed in bfloat16 or wider, within the bound.
A program may use at most 128 MiB of HBM per device.

v0:
```python
import math

import jax
import jax.numpy as jnp
from jax import lax
from jax.sharding import PartitionSpec as P

LAGS = 512
P_SIZE = 128
BS = 2
DESTS = 4


WATER = 0.5
EPSILON = 1e-06


def padded(block, sides, width):
    for axis, dim in sides:
        count = lax.axis_size(axis)
        forward = [(i, i + 1) for i in range(count - 1)]
        backward = [(target, source) for source, target in forward]
        low = lax.ppermute(
            lax.slice_in_dim(block, block.shape[dim] - width, None, axis=dim), axis, forward
        )
        high = lax.ppermute(lax.slice_in_dim(block, 0, width, axis=dim), axis, backward)
        block = jnp.concatenate([low, block, high], axis=dim)
    return block


def make_table(length):
    sample_ids = jnp.arange(length, dtype=jnp.int32)
    product = sample_ids[:, None] * sample_ids[None, :] % length
    angles = product.astype(jnp.float32) * (2.0 * math.pi / length)
    return jnp.concatenate([jnp.cos(angles), jnp.sin(angles)], axis=1).astype(jnp.bfloat16)


def toeplitz_blocks(extended):
    own_count = extended.shape[0]
    blocks = extended.reshape(own_count, -1, P_SIZE)
    block_pairs = jnp.concatenate([blocks[:, :-1], blocks[:, 1:]], axis=2)
    pair_count = block_pairs.shape[1]
    padded_pairs = jnp.pad(block_pairs, ((0, 0), (0, 0), (0, 1)))
    spread = jnp.broadcast_to(
        padded_pairs[:, :, None, :], (own_count, pair_count, P_SIZE, 2 * P_SIZE + 1)
    )
    spread = spread.reshape(own_count, pair_count, P_SIZE * (2 * P_SIZE + 1))[
        :, :, : P_SIZE * 2 * P_SIZE
    ]
    spread = spread.reshape(own_count, pair_count, P_SIZE, 2 * P_SIZE)
    return spread[:, :, :, P_SIZE:]


def on_device(records, owners):
    own_count, seg_len = records.shape
    seg_count = lax.axis_size("seg")
    window = seg_len * seg_count
    dft_table = make_table(seg_len)
    spectrum = jnp.dot(records, dft_table, preferred_element_type=jnp.float32)
    real_part = spectrum[:, :seg_len]
    imag_part = spectrum[:, seg_len:]
    magnitude = jnp.sqrt(real_part * real_part + imag_part * imag_part)
    amp_total = lax.psum(jnp.sum(magnitude, axis=1), "seg")
    water_level = WATER * amp_total / window + EPSILON
    flattened = (
        spectrum / (jnp.concatenate([magnitude, magnitude], axis=1) + water_level[:, None])
    ).astype(jnp.bfloat16)
    white_trace = lax.dot_general(
        flattened, dft_table, (((1,), (1,)), ((), ())), preferred_element_type=jnp.float32
    ) * (1.0 / seg_len)
    energy = lax.psum(jnp.sum(white_trace * white_trace, axis=1), "seg")
    whitened = (white_trace * lax.rsqrt(energy / window + EPSILON)[:, None]).astype(jnp.bfloat16)
    half_lags = LAGS // 2
    extended = padded(whitened, (("seg", 1),), half_lags)
    lagged = toeplitz_blocks(extended)
    pair_count = lagged.shape[1]
    sources = lax.axis_size("sta")
    block_count = own_count // BS
    slot_count = max(2, 2 * block_count * DESTS // sources)
    slot_ids = jnp.arange(slot_count, dtype=jnp.int32)
    everyone, all_owners = (
        lax.all_gather(whitened, "sta", axis=0, tiled=True),
        lax.all_gather(owners, "sta", axis=0, tiled=True),
    )
    my_index = lax.axis_index("sta")
    wanted = jnp.any(all_owners == my_index, axis=1).reshape(sources, block_count)
    wanted_count = wanted.astype(jnp.int32)
    slot_rank = jnp.cumsum(wanted_count, axis=1) - wanted_count
    selector = (wanted[:, None, :] & (slot_rank[:, None, :] == slot_ids[None, :, None])).astype(
        jnp.bfloat16
    )
    block_data = everyone.reshape(sources, block_count, BS * seg_len)
    received = (
        jnp.einsum("sqj,sjx->sqx", selector, block_data, preferred_element_type=jnp.float32)
        .astype(jnp.bfloat16)
        .reshape(-1, seg_len)
    )
    recv_rows = received.shape[0]
    shift_count = LAGS // P_SIZE
    seg_blocks = received.reshape(recv_rows, seg_len // P_SIZE, P_SIZE)
    padded_rows = jnp.pad(seg_blocks, ((0, 0), (shift_count - 1, shift_count - 1), (0, 0)))
    shifted = jnp.stack(
        [padded_rows[:, offset : offset + pair_count] for offset in range(shift_count)], axis=1
    )
    corr_scale = 1.0 / math.sqrt(window)
    product = jnp.einsum("ajui,bsji->basu", lagged, shifted, preferred_element_type=jnp.float32)
    stacked = lax.psum_scatter(
        (
            product.reshape(recv_rows // seg_count * lax.axis_size("seg"), own_count, LAGS)
            * corr_scale
        ).astype(jnp.bfloat16),
        "seg",
        scatter_dimension=0,
        tiled=True,
    )
    return (whitened, stacked)


def solution(mesh):
    return jax.shard_map(
        on_device,
        mesh=mesh,
        in_specs=(P("sta", "seg"), P("sta", None)),
        out_specs=(P("sta", "seg"), P("seg", "sta", None)),
        check_vma=False,
    )
```

profile of v0, /device:TPU:3, one launch (start us, length us, event | category | flops | bytes accessed | tf_op | source)
XLA Modules:
  0.0 282.9 jit_solution(3536200428975397832)
XLA Ops:
  7.2 66.7 %sine_convert_fusion = (bf16[2048,2048]{1,0:T(8,128)(2,1)S(1)}, bf16[2048,2048]{1,0:T(8,128)(2,1)S(1)}) fusion(), kind=kLoop, calls=%fused_computation.7 | loop fusion | flops 67108864 | bytes 16777216 | tf_op jit(solution)/shard_map/convert.1
  74.0 2.3 fusion.9
  76.3 0.9 copy-done.2
  77.2 2.5 copy-done.3
  79.7 0.2 fusion.36
  79.8 5.7 %psum.14 = f32[16]{0:T(128)S(1)} all-reduce(f32[16]{0:T(128)S(1)} %get-tuple-element.4), channel_id=1, replica_groups=mesh['sta'=8,'seg'=4] {'seg'}, use_global_device_ids=true, to_apply=%region_1.2 | all-reduce | flops 16 | bytes 128 | tf_op jit(solution)/shard_map/psum | solution.py:63
  85.6 8.3 %multiply_reduce_fusion = (f32[16]{0:T(128)S(1)}, f32[16,2048]{1,0:T(8,128)S(1)}) fusion(bf16[2048,2048]{1,0:T(8,128)(2,1)} %copy-done.2, bf16[2048,2048]{1,0:T(8,128)(2,1)} %copy-done.3, f32[16,4096]{1,0:T(8,128)S(1)} %fusion.9, f32[16,2048]{1,0:T(8,128)S(1)} %get-tuple-element.5, f32[16]{0:T(128)S(1)} %multiply_add_fusion), kind=kOutput, calls=%fused_computation.45 | convolution fusion | flops 302350336 | bytes 17301632 | tf_op jit(solution)/shard_map/dot_general | solution.py:68
  93.8 5.8 %psum.15 = f32[16]{0:T(128)S(1)} all-reduce(f32[16]{0:T(128)S(1)} %get-tuple-element.14), channel_id=1, replica_groups=mesh['sta'=8,'seg'=4] {'seg'}, use_global_device_ids=true, to_apply=%region_3.4 | all-reduce | flops 16 | bytes 128 | tf_op jit(solution)/shard_map/psum | solution.py:71
  99.7 1.3 collective-permute-start
  101.0 3.2 %collective-permute-start.1 = (bf16[16,256]{1,0:T(8,128)(2,1)S(1)}, bf16[16,256]{1,0:T(8,128)(2,1)S(1)}, u32[]{:S(2)}, u32[]{:S(2)}) collective-permute-start(bf16[16,256]{1,0:T(8,128)(2,1)S(1)} %get-tuple-element.13), channel_id=1, source_target_pairs={{1,0},{2,1},{3,2},{5,4},{6,5},{7,6},{9,8},{10,9},{11,10},{13,12},{... | collective-permute-start | bytes 24584 | tf_op jit(solution)/shard_map/ppermute | solution.py:26
  104.2 25.7 %all_gather.7 = bf16[128,2048]{1,0:T(8,128)(2,1)S(1)} all-gather(bf16[16,2048]{1,0:T(8,128)(2,1)S(1)} %multiply_convert_fusion), channel_id=1, replica_groups=mesh['sta'=8,'seg'=4] {'sta'}, dimensions={0}, use_global_device_ids=true | all-gather | bytes 589824 | tf_op jit(solution)/shard_map/all_gather | solution.py:82
  129.9 0.2 reshape.41
  130.1 22.1 %all-gather = s32[8,8,4]{1,2,0:T(4,128)S(1)} all-gather(s32[1,8,4]{1,2,0:T(4,128)S(1)} %bitcast.48), channel_id=1, replica_groups=mesh['sta'=8,'seg'=4] {'sta'}, dimensions={0}, use_global_device_ids=true | all-gather | bytes 1152 | tf_op jit(solution)/shard_map/all_gather | solution.py:83
  152.2 0.2 reduce_window_sum.11
  152.4 0.3 convolution_convert_fusion
  152.7 0.2 reshape_reshape.3
  153.1 0.6 fusion.18
  153.9 10.0 %broadcast_in_dim.2 = bf16[16,19,128,257]{3,2,0,1:T(8,128)(2,1)} broadcast(bf16[16,19,257]{2,0,1:T(8,128)(2,1)S(1)} %pad.9.clone), dimensions={0,1,3} | broadcast | bytes 20157024 | tf_op jit(solution)/shard_map/broadcast_in_dim | solution.py:44
  163.9 45.8 %reshape.43 = bf16[16,19,32896]{2,0,1:T(8,128)(2,1)} reshape(bf16[16,19,128,257]{3,2,0,1:T(8,128)(2,1)} %broadcast_in_dim.2) | data formatting | bytes 40001536 | tf_op jit(solution)/shard_map/reshape | solution.py:47
  209.7 6.7 %slice-done = bf16[16,19,32768]{2,0,1:T(8,128)(2,1)S(1)} async-done(((bf16[16,19,32896]{2,0,1:T(8,128)(2,1)}), bf16[16,19,32768]{2,0,1:T(8,128)(2,1)S(1)}, s32[]{:S(2)}) %slice-start) | async-done | bytes 19922968 | tf_op jit(solution)/shard_map/slice | solution.py:47
  216.4 9.5 %copy.19 = bf16[38,8,128,256]{3,2,1,0:T(8,128)(2,1)S(1)} copy(bf16[38,8,128,256]{3,1,2,0:T(8,128)(2,1)S(1)} %bitcast.45) | data formatting | bytes 39845888
  225.8 5.8 %fusion.17 = bf16[128,16,4,128]{0,3,1,2:T(8,128)(2,1)S(1)} fusion(bf16[128,1,19,128]{3,0,2,1:T(8,128)(2,1)S(1)} %get-tuple-element.9, bf16[128,1,19,128]{3,0,2,1:T(8,128)(2,1)S(1)} %get-tuple-element.8, bf16[128,1,19,128]{3,0,2,1:T(8,128)(2,1)S(1)} %get-tuple-element.7, bf16[128,1,19,128]{3,0,2,1:T(8,128)(2,1)S(1)} %get-tuple-element.6, ...), kind=kOutput, calls=%fused_computation.27 | convolution fusion | flops 5112332288 | bytes 14548992 | tf_op jit(solution)/shard_map/ajui,bsji->basu/dot_general | solution.py:106
  231.8 3.0 %copy.14 = bf16[128,16,512]{2,1,0:T(8,128)(2,1)} copy(bf16[128,16,512]{0,2,1:T(8,128)(2,1)S(1)} %bitcast.47) | data formatting | bytes 4194304 | tf_op jit(solution)/shard_map/convert_element_type | solution.py:111
  234.9 41.2 %reduce-scatter.2.cloned.1.call-done = bf16[32,16,512]{2,1,0:T(8,128)(2,1)} async-done(((bf16[128,16,512]{2,1,0:T(8,128)(2,1)}), bf16[32,16,512]{2,1,0:T(8,128)(2,1)}) %reduce-scatter.2.cloned.1.call-update) | async-done | bytes 524304 | tf_op jit(solution)/shard_map/reduce_scatter | solution.py:107
  (30 shorter events, 0.7 us)
Async XLA Ops:
  7.2 66.8 %copy-start = (bf16[16,2048]{1,0:T(8,128)(2,1)S(1)}, bf16[16,2048]{1,0:T(8,128)(2,1)}, u32[]{:S(2)}) copy-start(bf16[16,2048]{1,0:T(8,128)(2,1)} %param.2) | copy-start | bytes 196612
  7.2 268.9 %reduce-scatter.2.cloned.1.call-start = ((), (), s32[]{:S(2)}) async-start(), calls=%async_computation.1 | async-start | bytes 2621440 | tf_op jit(solution)/shard_map/reduce_scatter | solution.py:107
  74.0 3.2 %copy-start.2 = (bf16[2048,2048]{1,0:T(8,128)(2,1)}, bf16[2048,2048]{1,0:T(8,128)(2,1)S(1)}, u32[]{:S(2)}) copy-start(bf16[2048,2048]{1,0:T(8,128)(2,1)S(1)} %get-tuple-element.16) | copy-start | bytes 25165828
  74.0 5.7 %copy-start.3 = (bf16[2048,2048]{1,0:T(8,128)(2,1)}, bf16[2048,2048]{1,0:T(8,128)(2,1)S(1)}, u32[]{:S(2)}) copy-start(bf16[2048,2048]{1,0:T(8,128)(2,1)S(1)} %get-tuple-element.17) | copy-start | bytes 25165828
  85.6 44.5 %copy-start.5 = (s32[8,4]{0,1:T(4,128)S(1)}, s32[8,4]{0,1:T(4,128)}, u32[]{:S(2)}) copy-start(s32[8,4]{0,1:T(4,128)} %param.3) | copy-start | bytes 388
  99.7 64.2 %copy-start.4 = (bf16[16,2048]{1,0:T(8,128)(2,1)}, bf16[16,2048]{1,0:T(8,128)(2,1)S(1)}, u32[]{:S(2)}) copy-start(bf16[16,2048]{1,0:T(8,128)(2,1)S(1)} %multiply_convert_fusion) | copy-start | bytes 196612
  99.7 54.0 %collective-permute-start = (bf16[16,256]{1,0:T(8,128)(2,1)S(1)}, bf16[16,256]{1,0:T(8,128)(2,1)S(1)}, u32[]{:S(2)}, u32[]{:S(2)}) collective-permute-start(bf16[16,256]{1,0:T(8,128)(2,1)S(1)} %get-tuple-element.12), channel_id=1, source_target_pairs={{0,1},{1,2},{2,3},{4,5},{5,6},{6,7},{8,9},{9,10},{10,11},{12,13},{... | collective-permute-start | bytes 24584 | tf_op jit(solution)/shard_map/ppermute | solution.py:23
  101.0 52.7 %collective-permute-start.1 = (bf16[16,256]{1,0:T(8,128)(2,1)S(1)}, bf16[16,256]{1,0:T(8,128)(2,1)S(1)}, u32[]{:S(2)}, u32[]{:S(2)}) collective-permute-start(bf16[16,256]{1,0:T(8,128)(2,1)S(1)} %get-tuple-element.13), channel_id=1, source_target_pairs={{1,0},{2,1},{3,2},{5,4},{6,5},{7,6},{9,8},{10,9},{11,10},{13,12},{... | collective-permute-start | bytes 24584 | tf_op jit(solution)/shard_map/ppermute | solution.py:26
  209.7 6.7 %slice-start = ((bf16[16,19,32896]{2,0,1:T(8,128)(2,1)}), bf16[16,19,32768]{2,0,1:T(8,128)(2,1)S(1)}, s32[]{:S(2)}) async-start(bf16[16,19,32896]{2,0,1:T(8,128)(2,1)} %reshape.43), calls=%async_computation.2 | async-start | bytes 39845888 | tf_op jit(solution)/shard_map/slice | solution.py:47
  225.8 50.3 %copy-start.1 = (bf16[16,2048]{1,0:T(8,128)(2,1)S(1)}, bf16[16,2048]{1,0:T(8,128)(2,1)}, u32[]{:S(2)}) copy-start(bf16[16,2048]{1,0:T(8,128)(2,1)} %param.2) | copy-start | bytes 196612
Sparse Core Ops, SparseCore 0:
  235.0 41.0 reduce-scatter.1
where the time goes:
time: 287 us; the launch traced here: 283 us
  local copies, waits for them, and re-layouts  79.8 us (28%)
  other arithmetic  67.2 us (23%)
  blocking collectives  59.3 us (21%)
  waiting for transfers between devices  41.2 us (14%)
  matrix products  16.7 us (6%)
  between operations  14.2 us (5%)
  starting transfers between devices  4.49 us (2%)
    another operation x1, other arithmetic  66.7 us
    reshape x1, local copies, waits for them, and re-layouts, toeplitz_blocks(): spread.reshape(own_count, pair_count, P_SIZE * (2 * P_SIZE + 1))  45.8 us
    reduce_scatter x1, waiting for transfers between devices, on_device(): lax.psum_scatter((product.reshape(recv_rows // seg_count * lax.axis_size(...  41.2 us
    all_gather x1, blocking collectives, on_device(): lax.all_gather(whitened, 'sta', axis=0, tiled=True)  25.7 us
    all_gather x1, blocking collectives, on_device(): lax.all_gather(owners, 'sta', axis=0, tiled=True)  22.1 us
    unnamed x14, local copies, waits for them, and re-layouts  12.9 us
    broadcast_in_dim x1, local copies, waits for them, and re-layouts, toeplitz_blocks(): jnp.broadcast_to(padded_pairs[:, :, None, :], (own_count, pair_count, P_S...  9.97 us
    dot_general x1, matrix products, on_device(): lax.dot_general(flattened, dft_table, (((1,), (1,)), ((), ())), preferred...  8.27 us
  transfers between devices with their start and end apart: 3, of which 1 were waited for; matrix products, arithmetic and copies ran while one was open for 1% of the time, Pallas kernels for 0%

commit v1 on v0

v1 whole, which is shorter than its diff:
```python
import functools
import math

import jax
import jax.numpy as jnp
import numpy as np
from jax import lax
from jax.experimental import pallas as pl
from jax.experimental.pallas import tpu as pltpu
from jax.sharding import PartitionSpec as P

LAGS = 512
LANES = 128
BS = 2
DESTS = 4
SUB = 32

WATER = 0.5
EPSILON = 1e-06
MESH = pl.DeviceIdType.MESH


def conj(value):
    return value[0], -value[1]


def real_dft(slabs):
    n = len(slabs)
    if n == 2:
        zero = jnp.zeros_like(slabs[0])
        return [(slabs[0] + slabs[1], zero), (slabs[0] - slabs[1], zero)]
    even, odd = real_dft(slabs[::2]), real_dft(slabs[1::2])
    half = n // 2

    def at(values, k):
        k %= half
        return values[k] if k <= half // 2 else conj(values[half - k])

    result = []
    for k in range(half + 1):
        c, s = math.cos(2 * math.pi * k / n), math.sin(2 * math.pi * k / n)
        (er, ei), (pr, pi) = at(even, k), at(odd, k)
        if k == 0:
            result.append((er + pr, ei + pi))
        elif k == half:
            result.append((er - pr, ei - pi))
        elif 4 * k == n:
            result.append((er - pi, ei + pr))
        else:
            result.append((er + c * pr - s * pi, ei + s * pr + c * pi))
    return result


def real_inverse(values, n):
    if n == 2:
        return [values[0][0] + values[1][0], values[0][0] - values[1][0]]
    half = n // 2
    even, odd = [], []
    for k in range(half // 2 + 1):
        (ar, ai), (br, bi) = values[k], conj(values[half - k])
        even.append((ar + br, ai + bi))
        dr, di = ar - br, ai - bi
        c, s = math.cos(2 * math.pi * k / n), math.sin(2 * math.pi * k / n)
        if k == 0:
            odd.append((dr, di))
        elif 4 * k == n:
            odd.append((di, -dr))
        else:
            odd.append((dr * c + di * s, di * c - dr * s))
    slabs = [None] * n
    slabs[::2] = real_inverse(even, half)
    slabs[1::2] = real_inverse(odd, half)
    return slabs


def tables(seg_len):
    lanes = np.arange(LANES)
    angle = 2 * np.pi * (np.outer(lanes, lanes) % LANES) / LANES
    c, s = np.cos(angle), np.sin(angle)
    forward = np.block([[c, s], [-s, c]])
    count = seg_len // LANES // 2 + 1
    turn = 2 * np.pi * np.outer(np.arange(count), lanes) / seg_len
    twiddle = np.stack([np.cos(turn), np.sin(turn)]).astype(np.float32)
    return (
        jnp.asarray(twiddle),
        jnp.asarray(forward, jnp.bfloat16),
        jnp.asarray(forward.T, jnp.bfloat16),
    )


def whiten(slabs, seg_count, own_count, twiddle, forward, backward):
    n1 = len(slabs)
    seg_len = n1 * LANES
    window = seg_len * seg_count
    rows = seg_count * own_count

    def over_window(value):
        total = value[:own_count]
        for g in range(1, seg_count):
            total = total + value[g * own_count : (g + 1) * own_count]
        return jnp.sum(total, axis=1, keepdims=True)

    def every_segment(value):
        return jnp.concatenate([value] * seg_count, axis=0)

    first = real_dft(slabs)
    turned = []
    for k, (re, im) in enumerate(first):
        if k:
            c, s = twiddle[0, k : k + 1, :], twiddle[1, k : k + 1, :]
            re, im = re * c - im * s, re * s + im * c
        turned.append(jnp.concatenate([re, im], axis=1).astype(jnp.bfloat16))
    spectrum = jnp.dot(
        jnp.concatenate(turned, axis=0), forward, preferred_element_type=jnp.float32
    )
    parts, total = [], None
    for k in range(len(first)):
        re = spectrum[k * rows : (k + 1) * rows, :LANES]
        im = spectrum[k * rows : (k + 1) * rows, LANES:]
        magnitude = jnp.sqrt(re * re + im * im)
        parts.append((re, im, magnitude))
        term = magnitude if k in (0, n1 // 2) else 2.0 * magnitude
        total = term if total is None else total + term
    level = every_segment(WATER * over_window(total) / window + EPSILON)
    flat = []
    for re, im, magnitude in parts:
        inverse = 1.0 / (magnitude + level)
        flat.append(jnp.concatenate([re * inverse, im * inverse], axis=1).astype(jnp.bfloat16))
    back = jnp.dot(
        jnp.concatenate(flat, axis=0), backward, preferred_element_type=jnp.float32
    )
    turned = []
    for k in range(len(first)):
        re = back[k * rows : (k + 1) * rows, :LANES]
        im = back[k * rows : (k + 1) * rows, LANES:]
        if k:
            c, s = twiddle[0, k : k + 1, :], twiddle[1, k : k + 1, :]
            re, im = re * c + im * s, im * c - re * s
        turned.append((re, im))
    trace = [slab * (1.0 / seg_len) for slab in real_inverse(turned, n1)]
    squares = trace[0] * trace[0]
    for slab in trace[1:]:
        squares = squares + slab * slab
    scale = every_segment(lax.rsqrt(over_window(squares) / window + EPSILON))
    return [slab * scale for slab in trace]


def gather_kernel(
    n_sta,
    n_seg,
    records,
    owners,
    twiddle,
    forward,
    backward,
    white,
    own,
    received,
    held,
    seg_send,
    seg_recv,
    z_send,
    z_recv,
    y_send,
    y_recv,
):
    depth = n_sta // n_seg
    planes = n_seg
    own_count, seg_len = records.shape
    n1 = seg_len // LANES
    g, s = lax.axis_index("seg"), lax.axis_index("sta")
    z, y = s // depth, s % depth

    barrier = pltpu.get_barrier_semaphore()
    for d in range(1, n_seg):
        pl.semaphore_signal(barrier, inc=1, device_id={"seg": (g + d) % n_seg}, device_id_type=MESH)
    for d in range(1, depth):
        pl.semaphore_signal(
            barrier, inc=1, device_id={"sta": z * depth + (y + d) % depth}, device_id_type=MESH
        )

    @pl.when(z > 0)
    def _():
        pl.semaphore_signal(barrier, inc=1, device_id={"sta": s - depth}, device_id_type=MESH)

    @pl.when(z < planes - 1)
    def _():
        pl.semaphore_signal(barrier, inc=1, device_id={"sta": s + depth}, device_id_type=MESH)

    below, above = (z + planes - 1) // planes, (2 * planes - 2 - z) // planes
    pl.semaphore_wait(barrier, n_seg - 1 + depth - 1 + below + above)

    copies = []
    for d in range(1, n_seg):
        copy = pltpu.make_async_remote_copy(
            src_ref=records,
            dst_ref=held.at[g],
            send_sem=seg_send.at[d - 1],
            recv_sem=seg_recv.at[d - 1],
            device_id={"seg": (g + d) % n_seg},
            device_id_type=MESH,
        )
        copy.start()
        copies.append(copy)
    held[g] = records[...]
    for copy in copies:
        copy.wait()

    slabs = []
    for t in range(n1):
        slabs.append(
            jnp.concatenate(
                [held[j, :, t * LANES : (t + 1) * LANES].astype(jnp.float32) for j in range(n_seg)],
                axis=0,
            )
        )
    result = whiten(slabs, n_seg, own_count, twiddle, forward[...], backward[...])
    for t in range(n1):
        rounded = result[t].astype(jnp.bfloat16)
        for j in range(n_seg):
            own[j * n1 + t] = rounded[j * own_count : (j + 1) * own_count]
    own[n_seg * n1] = owners[...]

    @pl.when(z == g)
    def _():
        received[y] = own[...]

    up = jnp.logical_and(z >= g, z < planes - 1)
    down = jnp.logical_and(z <= g, z > 0)

    def along_z(j, target):
        size = n1 + (1 if j == n_seg - 1 else 0)
        part = received.at[y, pl.ds(j * n1, size)]
        return pltpu.make_async_remote_copy(
            src_ref=part,
            dst_ref=part,
            send_sem=z_send.at[j],
            recv_sem=z_recv.at[j],
            device_id={"sta": target},
            device_id_type=MESH,
        )

    def along_z_up(j):
        return along_z(j, s + depth)

    def along_z_down(j):
        size = n1 + (1 if j == n_seg - 1 else 0)
        part = received.at[y, pl.ds(j * n1, size)]
        return pltpu.make_async_remote_copy(
            src_ref=part,
            dst_ref=part,
            send_sem=z_send.at[n_seg + j],
            recv_sem=z_recv.at[j],
            device_id={"sta": s - depth},
            device_id_type=MESH,
        )

    def along_y(j, d):
        size = n1 + (1 if j == n_seg - 1 else 0)
        part = received.at[y, pl.ds(j * n1, size)]
        return pltpu.make_async_remote_copy(
            src_ref=part,
            dst_ref=part,
            send_sem=y_send.at[d - 1, j],
            recv_sem=y_recv.at[d - 1, j],
            device_id={"sta": z * depth + (y + d) % depth},
            device_id_type=MESH,
        )

    for j in range(n_seg):

        @pl.when(z != g)
        def _():
            along_z_up(j).wait_recv()

        @pl.when(up)
        def _():
            along_z_up(j).start()

        @pl.when(down)
        def _():
            along_z_down(j).start()

        for d in range(1, depth):
            along_y(j, d).start()
    for t in range(n1):
        white[:, t * LANES : (t + 1) * LANES] = own[g * n1 + t]
    for j in range(n_seg):
        for d in range(1, depth):
            along_y(j, d).wait()

        @pl.when(up)
        def _():
            along_z_up(j).wait_send()

        @pl.when(down)
        def _():
            along_z_down(j).wait_send()


def lag_kernel(n_sta, n_seg, slots, own, received, flip, out, ext, rec, left, sums):
    depth = n_sta // n_seg
    nk, own_count = own.shape[0] - 1, own.shape[1]
    stations = depth * own_count
    parts = LANES // SUB
    tiles = LAGS // LANES + 1
    edge = LAGS // 2 // LANES
    me = lax.axis_index("sta").astype(jnp.float32)
    lane = lax.broadcasted_iota(jnp.int32, (own_count, LANES), 1)

    zero = jnp.zeros((own_count, LANES), jnp.float32)

    def padded(k):
        inside = 0 <= k - edge < nk
        return own[k - edge].astype(jnp.float32) if inside else zero

    def spread(k, now, later):
        ext[0, k] = now
        for c in range(1, parts):
            shift = LANES - SUB * c
            ext[c, k] = jnp.where(
                lane < shift, pltpu.roll(now, shift, 1), pltpu.roll(later, shift, 1)
            )

    for k in list(range(edge)) + list(range(nk + edge - 1, nk + tiles - 1)):
        spread(k, padded(k), padded(k + 1))

    def inner(k, carry):
        spread(k, own[k - edge].astype(jnp.float32), own[k - edge + 1].astype(jnp.float32))
        return carry

    lax.fori_loop(edge, nk + edge - 1, inner, 0)

    for y in range(depth):
        rec[...] = received[y, :nk].astype(jnp.float32)
        for b in range(own_count):
            turned = rec[:, b, :].T
            for c in range(parts):
                left[:, y * own_count + b, c * nk : (c + 1) * nk] = turned[
                    c * SUB : (c + 1) * SUB
                ]
    lhs = left[...].reshape(SUB * stations, parts * nk).astype(jnp.bfloat16)

    shape = (stations, stations)
    row = lax.broadcasted_iota(jnp.int32, shape, 0)
    station = lax.broadcasted_iota(jnp.int32, (1, stations), 1)
    source, block = station // own_count, station % own_count // BS
    number = lax.broadcasted_iota(jnp.int32, (own_count, stations), 0)
    wanted = jnp.zeros((1, stations), jnp.float32)
    rank = jnp.zeros((1, stations), jnp.float32)
    for y in range(depth):
        names = received[y, nk].astype(jnp.float32)
        named = jnp.max(
            jnp.where(jnp.logical_and(lane < DESTS, names == me), 1.0, 0.0), axis=1, keepdims=True
        )
        named = jnp.where(source == y, named, 0.0)
        wanted = wanted + jnp.sum(jnp.where(number == block, named, 0.0), axis=0, keepdims=True)
        rank = rank + jnp.sum(jnp.where(number < block, named, 0.0), axis=0, keepdims=True)
    slot = row // BS % slots
    hit = jnp.logical_and(row // (BS * slots) == source, row % BS == station % BS)
    hit = jnp.logical_and(hit, slot == rank.astype(jnp.int32))
    select = jnp.where(hit, wanted, 0.0).astype(jnp.bfloat16)
    rows = out.shape[0]
    window = nk * LANES
    scale = 1.0 / math.sqrt(window)

    for a in range(own_count):
        rhs = jnp.concatenate(
            [
                jnp.concatenate([ext[c, v : v + nk, a, :] for v in range(tiles)], axis=1)
                for c in range(parts)
            ],
            axis=0,
        ).astype(jnp.bfloat16)
        gram = jnp.dot(lhs, rhs, preferred_element_type=jnp.float32)
        terms = [gram[i * stations : (i + 1) * stations] for i in range(SUB)]
        width = tiles * LANES
        step = 1
        while len(terms) > 1:
            terms = [
                terms[i] + pltpu.roll(terms[i + 1], width - step, 1)
                for i in range(0, len(terms), 2)
            ]
            step *= 2
        total = pltpu.roll(terms[0], width - 1, 1)[:, :LAGS] * scale
        sums[a] = jnp.dot(
            select, total.astype(jnp.bfloat16), preferred_element_type=jnp.float32
        ).astype(jnp.bfloat16)[:rows]
    for a in range(own_count):
        out[:, a, :] = jnp.dot(
            sums[a], flip[...], preferred_element_type=jnp.float32
        ).astype(jnp.bfloat16)


def on_device(n_sta, n_seg, records, owners):
    own_count, seg_len = records.shape
    depth = n_sta // n_seg
    n1 = seg_len // LANES
    nk = n1 * n_seg
    blocks = own_count // BS
    slots = max(2, 2 * blocks * DESTS // n_sta)
    names = jnp.pad(
        owners.astype(jnp.bfloat16), ((0, own_count - blocks), (0, LANES - DESTS))
    )
    vmem = pl.BlockSpec(memory_space=pltpu.VMEM)
    white, own, received = pl.pallas_call(
        functools.partial(gather_kernel, n_sta, n_seg),
        out_shape=(
            jax.ShapeDtypeStruct((own_count, seg_len), jnp.bfloat16),
            jax.ShapeDtypeStruct((nk + 1, own_count, LANES), jnp.bfloat16),
            jax.ShapeDtypeStruct((depth, nk + 1, own_count, LANES), jnp.bfloat16),
        ),
        in_specs=[vmem] * 5,
        out_specs=(vmem,) * 3,
        scratch_shapes=[
            pltpu.VMEM((n_seg, own_count, seg_len), jnp.bfloat16),
            pltpu.SemaphoreType.DMA((n_seg - 1,)),
            pltpu.SemaphoreType.DMA((n_seg - 1,)),
            pltpu.SemaphoreType.DMA((2 * n_seg,)),
            pltpu.SemaphoreType.DMA((n_seg,)),
            pltpu.SemaphoreType.DMA((depth - 1, n_seg)),
            pltpu.SemaphoreType.DMA((depth - 1, n_seg)),
        ],
        compiler_params=pltpu.CompilerParams(
            collective_id=0, has_side_effects=True, vmem_limit_bytes=32 * 2**20
        ),
        name="whiten_and_gather",
    )(records, names, *tables(seg_len))
    stations = depth * own_count
    rows = depth * slots * BS
    flip = jnp.asarray(np.eye(LAGS)[::-1], jnp.bfloat16)
    parts = LANES // SUB
    tiles = LAGS // LANES + 1
    correlations = pl.pallas_call(
        functools.partial(lag_kernel, n_sta, n_seg, slots),
        out_shape=jax.ShapeDtypeStruct((rows, own_count, LAGS), jnp.bfloat16),
        in_specs=[vmem] * 3,
        out_specs=vmem,
        scratch_shapes=[
            pltpu.VMEM((parts, nk + tiles - 1, own_count, LANES), jnp.float32),
            pltpu.VMEM((nk, own_count, LANES), jnp.float32),
            pltpu.VMEM((SUB, stations, parts * nk), jnp.float32),
            pltpu.VMEM((own_count, rows, LAGS), jnp.bfloat16),
        ],
        compiler_params=pltpu.CompilerParams(vmem_limit_bytes=48 * 2**20),
        name="correlate",
    )(own, received, flip)
    return white, correlations


def solution(mesh):
    return jax.shard_map(
        functools.partial(on_device, mesh.shape["sta"], mesh.shape["seg"]),
        mesh=mesh,
        in_specs=(P("sta", "seg"), P("sta", None)),
        out_specs=(P("sta", "seg"), P("seg", "sta", None)),
        check_vma=False,
    )
```

time: 287 us -> 61.4 us (0.21); the launches traced: 283 us -> 61.1 us
  local copies, waits for them, and re-layouts: 79.8 us -> 5.14 us
  other arithmetic: 67.2 us -> 0.69 us
  blocking collectives: 59.3 us -> 0 us
  Pallas kernels: 0 us -> 54.6 us
  waiting for transfers between devices: 41.2 us -> 0 us
  matrix products: 16.7 us -> 0 us
  between operations: 14.2 us -> 0.65 us
  starting transfers between devices: 4.49 us -> 0 us
    another operation x2 -> x0, other arithmetic: 66.9 us -> none
    pallas_call x0 -> x2, Pallas kernels: none -> 54.6 us  [the longest x1 31.7 us: on_device(): pl.pallas_call(functools.partial(lag_kernel, n_sta, n_seg, slots), out_sh...]
    all_gather x2 -> x0, blocking collectives: 47.8 us -> none  [the longest x1 25.7 us: on_device(): lax.all_gather(whitened, 'sta', axis=0, tiled=True)]
    reshape x3 -> x0, local copies, waits for them, and re-layouts: 46 us -> none  [the longest x1 45.8 us: toeplitz_blocks(): spread.reshape(own_count, pair_count, P_SIZE * (2 * P_SIZE + 1))]
    reduce_scatter x1 -> x0, waiting for transfers between devices: 41.2 us -> none  [on_device(): lax.psum_scatter((product.reshape(recv_rows // seg_count * lax.axis_size(...]
    dot_general x4 -> x0, matrix products: 16.7 us -> none  [the longest x1 8.27 us: on_device(): lax.dot_general(flattened, dft_table, (((1,), (1,)), ((), ())), preferred...]
    psum x2 -> x0, blocking collectives: 11.5 us -> none  [the longest x1 5.76 us: on_device(): energy = lax.psum(jnp.sum(white_trace * white_trace, axis=1), 'seg')]
    broadcast_in_dim x1 -> x0, local copies, waits for them, and re-layouts: 9.97 us -> none  [toeplitz_blocks(): jnp.broadcast_to(padded_pairs[:, :, None, :], (own_count, pair_count, P_S...]
  transfers between devices with their start and end apart: 3 -> 0, of which waited for: 1 -> 0; matrix products, arithmetic and copies ran while one was open for 1% -> 0% of each run, Pallas kernels for 0% -> 0%
where the time goes in v1:
time: 61.4 us; the launch traced here: 61.1 us
  Pallas kernels  54.6 us (89%)
  local copies, waits for them, and re-layouts  5.14 us (8%)
  other arithmetic  0.69 us (1%)
  between operations  0.65 us (1%)
    pallas_call x1, Pallas kernels, on_device(): pl.pallas_call(functools.partial(lag_kernel, n_sta, n_seg, slots), out_sh...  31.7 us
    pallas_call x1, Pallas kernels, on_device(): pl.pallas_call(functools.partial(gather_kernel, n_sta, n_seg), out_shape=...  23 us
    unnamed x11, local copies, waits for them, and re-layouts  5.03 us

profile of v1, /device:TPU:3, one launch (start us, length us, event | category | flops | bytes accessed | tf_op | source)
XLA Modules:
  0.0 61.1 jit_solution(4187586788701549694)
XLA Ops:
  0.6 0.7 %convert_element_type.5 = bf16[8,4]{0,1:T(4,128)(2,1)S(1)} convert(s32[8,4]{0,1:T(4,128)} %param.7) | non-fusion elementwise | flops 32 | bytes 192 | tf_op jit(solution)/shard_map/convert_element_type | solution.py:403
  1.3 0.1 copy.9
  1.4 0.0 copy-start.1
  1.4 0.9 %copy-done.1 = bf16[256,256]{1,0:T(8,128)(2,1)S(1)} copy-done((bf16[256,256]{1,0:T(8,128)(2,1)S(1)}, bf16[256,256]{1,0:T(8,128)(2,1)}, u32[]{:S(2)}) %copy-start.1) | copy-done | bytes 131096
  2.3 0.0 copy-start.2
  2.3 0.9 %copy-done.2 = bf16[256,256]{1,0:T(8,128)(2,1)S(1)} copy-done((bf16[256,256]{1,0:T(8,128)(2,1)S(1)}, bf16[256,256]{1,0:T(8,128)(2,1)}, u32[]{:S(2)}) %copy-start.2) | copy-done | bytes 131096
  3.2 0.0 copy-start.3
  3.2 0.8 %copy-done.3 = bf16[16,2048]{1,0:T(8,128)(2,1)S(1)} copy-done((bf16[16,2048]{1,0:T(8,128)(2,1)S(1)}, bf16[16,2048]{1,0:T(8,128)(2,1)}, u32[]{:S(2)}) %copy-start.3) | copy-done | bytes 65560
  4.1 0.0 copy-start.4
  4.1 0.7 %copy-done.4 = f32[2,9,128]{2,1,0:T(8,128)S(1)} copy-done((f32[2,9,128]{2,1,0:T(8,128)S(1)}, f32[2,9,128]{2,1,0:T(8,128)}, u32[]{:S(2)}) %copy-start.4) | copy-done | bytes 9240
  4.8 23.0 %whiten_and_gather.1 = (bf16[16,2048]{1,0:T(8,128)(2,1)S(1)}, bf16[65,16,128]{2,1,0:T(8,128)(2,1)S(1)}, bf16[2,65,16,128]{3,2,1,0:T(8,128)(2,1)S(1)}) custom-call(bf16[16,2048]{1,0:T(8,128)(2,1)S(1)} %copy-done.3, bf16[16,128]{1,0:T(8,128)(2,1)S(1)} %pad.4.owners, f32[2,9,128]{2,1,0:T(8,128)S(1)} %copy-done.4, bf16[256,256]{1,0:T(8,128)(2,1)S(1)} %copy-done.2, ...), custom_call_target="tpu_custom_call" | custom-call | tf_op jit(solution)/shard_map/whiten_and_gather/pallas_call | solution.py:406
  27.8 0.0 copy-start
  27.8 1.0 %copy-done = bf16[512,512]{1,0:T(8,128)(2,1)S(1)} copy-done((bf16[512,512]{1,0:T(8,128)(2,1)S(1)}, bf16[512,512]{1,0:T(8,128)(2,1)}, u32[]{:S(2)}) %copy-start) | copy-done | bytes 524312
  28.8 31.7 %correlate.1 = bf16[32,16,512]{2,1,0:T(8,128)(2,1)} custom-call(bf16[65,16,128]{2,1,0:T(8,128)(2,1)S(1)} %get-tuple-element.6.own, bf16[2,65,16,128]{3,2,1,0:T(8,128)(2,1)S(1)} %get-tuple-element.7.received, bf16[512,512]{1,0:T(8,128)(2,1)S(1)} %copy-done), custom_call_target="tpu_custom_call" | custom-call | tf_op jit(solution)/shard_map/correlate/pallas_call | solution.py:434
  60.5 0.6 %copy.11 = bf16[16,2048]{1,0:T(8,128)(2,1)} copy(bf16[16,2048]{1,0:T(8,128)(2,1)S(1)} %get-tuple-element.10) | data formatting | bytes 131072
  (1 shorter events, 0.0 us)
Async XLA Ops:
  1.4 0.9 %copy-start.1 = (bf16[256,256]{1,0:T(8,128)(2,1)S(1)}, bf16[256,256]{1,0:T(8,128)(2,1)}, u32[]{:S(2)}) copy-start(bf16[256,256]{1,0:T(8,128)(2,1)} %constant.13.clone.backward) | copy-start | bytes 393220
  2.3 0.9 %copy-start.2 = (bf16[256,256]{1,0:T(8,128)(2,1)S(1)}, bf16[256,256]{1,0:T(8,128)(2,1)}, u32[]{:S(2)}) copy-start(bf16[256,256]{1,0:T(8,128)(2,1)} %constant.12.clone.forward) | copy-start | bytes 393220
  3.2 0.8 %copy-start.3 = (bf16[16,2048]{1,0:T(8,128)(2,1)S(1)}, bf16[16,2048]{1,0:T(8,128)(2,1)}, u32[]{:S(2)}) copy-start(bf16[16,2048]{1,0:T(8,128)(2,1)} %records.1) | copy-start | bytes 196612
  4.1 0.7 %copy-start.4 = (f32[2,9,128]{2,1,0:T(8,128)S(1)}, f32[2,9,128]{2,1,0:T(8,128)}, u32[]{:S(2)}) copy-start(f32[2,9,128]{2,1,0:T(8,128)} %constant.11.clone.twiddle) | copy-start | bytes 27652
  27.8 1.0 %copy-start = (bf16[512,512]{1,0:T(8,128)(2,1)S(1)}, bf16[512,512]{1,0:T(8,128)(2,1)}, u32[]{:S(2)}) copy-start(bf16[512,512]{1,0:T(8,128)(2,1)} %constant.14.clone.flip) | copy-start | bytes 1572868

commit v2 on v1

--- a/solution.py
+++ b/solution.py
@@ -13,7 +13,7 @@
 LANES = 128
 BS = 2
 DESTS = 4
-SUB = 32
+SUB = 16
 
 WATER = 0.5
 EPSILON = 1e-06
@@ -150,13 +150,18 @@
     n_seg,
     records,
     owners,
-    twiddle,
-    forward,
-    backward,
+    twiddle_in,
+    forward_in,
+    backward_in,
     white,
     own,
     received,
     held,
+    twiddle,
+    forward,
+    backward,
+    names,
+    table_sem,
     seg_send,
     seg_recv,
     z_send,
@@ -171,6 +176,21 @@
     g, s = lax.axis_index("seg"), lax.axis_index("sta")
     z, y = s // depth, s % depth
 
+    fetches = [
+        pltpu.make_async_copy(source, target, table_sem.at[i])
+        for i, (source, target) in enumerate(
+            (
+                (records, held.at[g]),
+                (twiddle_in, twiddle),
+                (forward_in, forward),
+                (backward_in, backward),
+            )
+        )
+    ]
+    for fetch in fetches:
+        fetch.start()
+    names[...] = jnp.zeros_like(names)
+    names[: owners.shape[0], : owners.shape[1]] = owners[...].astype(jnp.float32)
     barrier = pltpu.get_barrier_semaphore()
     for d in range(1, n_seg):
         pl.semaphore_signal(barrier, inc=1, device_id={"seg": (g + d) % n_seg}, device_id_type=MESH)
@@ -202,7 +222,8 @@
         )
         copy.start()
         copies.append(copy)
-    held[g] = records[...]
+    for fetch in fetches:
+        fetch.wait()
     for copy in copies:
         copy.wait()
 
@@ -219,7 +240,7 @@
         rounded = result[t].astype(jnp.bfloat16)
         for j in range(n_seg):
             own[j * n1 + t] = rounded[j * own_count : (j + 1) * own_count]
-    own[n_seg * n1] = owners[...]
+    own[n_seg * n1] = names[...].astype(jnp.bfloat16)
 
     @pl.when(z == g)
     def _():
@@ -298,98 +319,130 @@
             along_z_down(j).wait_send()
 
 
-def lag_kernel(n_sta, n_seg, slots, own, received, flip, out, ext, rec, left, sums):
+def lag_kernel(n_sta, n_seg, slots, own, received, out, flat, series, turned, rec, left, tails, sums, order):
     depth = n_sta // n_seg
     nk, own_count = own.shape[0] - 1, own.shape[1]
     stations = depth * own_count
     parts = LANES // SUB
-    tiles = LAGS // LANES + 1
+    tiles = LAGS // LANES
     edge = LAGS // 2 // LANES
+    per_tile = LANES // SUB
     me = lax.axis_index("sta").astype(jnp.float32)
-    lane = lax.broadcasted_iota(jnp.int32, (own_count, LANES), 1)
-
-    zero = jnp.zeros((own_count, LANES), jnp.float32)
-
-    def padded(k):
-        inside = 0 <= k - edge < nk
-        return own[k - edge].astype(jnp.float32) if inside else zero
-
-    def spread(k, now, later):
-        ext[0, k] = now
-        for c in range(1, parts):
-            shift = LANES - SUB * c
-            ext[c, k] = jnp.where(
-                lane < shift, pltpu.roll(now, shift, 1), pltpu.roll(later, shift, 1)
-            )
-
-    for k in list(range(edge)) + list(range(nk + edge - 1, nk + tiles - 1)):
-        spread(k, padded(k), padded(k + 1))
-
-    def inner(k, carry):
-        spread(k, own[k - edge].astype(jnp.float32), own[k - edge + 1].astype(jnp.float32))
-        return carry
-
-    lax.fori_loop(edge, nk + edge - 1, inner, 0)
+
+    flat[...] = own[:nk].astype(jnp.float32)
+    series[...] = jnp.zeros_like(series)
+    for a in range(own_count):
+        series[a, edge : edge + nk] = flat[:, a, :]
 
     for y in range(depth):
         rec[...] = received[y, :nk].astype(jnp.float32)
         for b in range(own_count):
-            turned = rec[:, b, :].T
-            for c in range(parts):
-                left[:, y * own_count + b, c * nk : (c + 1) * nk] = turned[
-                    c * SUB : (c + 1) * SUB
-                ]
+            across = rec[:, b, :].T
+            left[:, y * own_count + b, :] = jnp.concatenate(
+                [across[c * SUB : (c + 1) * SUB] for c in range(parts)], axis=1
+            )
     lhs = left[...].reshape(SUB * stations, parts * nk).astype(jnp.bfloat16)
+
+    lane = lax.broadcasted_iota(jnp.int32, (nk, LANES), 1)
+    for first in range(0, own_count, per_tile):
+        pieces = []
+        for c in range(parts):
+            piece = jnp.zeros((nk, LANES), jnp.float32)
+            for q in range(per_tile):
+                shift = (SUB * q - SUB * c - 1) % LANES
+                moved = series[first + q, tiles : tiles + nk]
+                moved = pltpu.roll(moved, shift, 1) if shift else moved
+                piece = jnp.where(lane // SUB == q, moved, piece)
+            pieces.append(piece)
+        tails[first // per_tile] = jnp.dot(
+            lhs,
+            jnp.concatenate(pieces, axis=0).astype(jnp.bfloat16),
+            preferred_element_type=jnp.float32,
+        )
 
     shape = (stations, stations)
     row = lax.broadcasted_iota(jnp.int32, shape, 0)
-    station = lax.broadcasted_iota(jnp.int32, (1, stations), 1)
+    station = lax.broadcasted_iota(jnp.int32, shape, 1)
     source, block = station // own_count, station % own_count // BS
-    number = lax.broadcasted_iota(jnp.int32, (own_count, stations), 0)
-    wanted = jnp.zeros((1, stations), jnp.float32)
-    rank = jnp.zeros((1, stations), jnp.float32)
+    wide = (LANES, stations)
+    number = lax.broadcasted_iota(jnp.int32, wide, 0)
+    wide_station = lax.broadcasted_iota(jnp.int32, wide, 1)
+    wide_block = wide_station % own_count // BS
+    entry = lax.broadcasted_iota(jnp.int32, (own_count, LANES), 0)
+    wanted = jnp.zeros(shape, jnp.float32)
+    rank = jnp.zeros(shape, jnp.float32)
     for y in range(depth):
         names = received[y, nk].astype(jnp.float32)
         named = jnp.max(
-            jnp.where(jnp.logical_and(lane < DESTS, names == me), 1.0, 0.0), axis=1, keepdims=True
-        )
-        named = jnp.where(source == y, named, 0.0)
-        wanted = wanted + jnp.sum(jnp.where(number == block, named, 0.0), axis=0, keepdims=True)
-        rank = rank + jnp.sum(jnp.where(number < block, named, 0.0), axis=0, keepdims=True)
-    slot = row // BS % slots
+            jnp.where(jnp.logical_and(entry < DESTS, names == me), 1.0, 0.0), axis=0, keepdims=True
+        )
+        named = jnp.broadcast_to(named, (stations, LANES)).astype(jnp.bfloat16)
+        here = wide_station // own_count == y
+        same = jnp.where(jnp.logical_and(here, number == wide_block), 1.0, 0.0)
+        before = jnp.where(jnp.logical_and(here, number < wide_block), 1.0, 0.0)
+        wanted += jnp.dot(named, same.astype(jnp.bfloat16), preferred_element_type=jnp.float32)
+        rank += jnp.dot(named, before.astype(jnp.bfloat16), preferred_element_type=jnp.float32)
+    slot = (row // BS % slots).astype(jnp.float32)
     hit = jnp.logical_and(row // (BS * slots) == source, row % BS == station % BS)
-    hit = jnp.logical_and(hit, slot == rank.astype(jnp.int32))
+    hit = jnp.logical_and(hit, slot == rank)
     select = jnp.where(hit, wanted, 0.0).astype(jnp.bfloat16)
     rows = out.shape[0]
     window = nk * LANES
     scale = 1.0 / math.sqrt(window)
-
-    for a in range(own_count):
-        rhs = jnp.concatenate(
-            [
-                jnp.concatenate([ext[c, v : v + nk, a, :] for v in range(tiles)], axis=1)
-                for c in range(parts)
-            ],
-            axis=0,
-        ).astype(jnp.bfloat16)
-        gram = jnp.dot(lhs, rhs, preferred_element_type=jnp.float32)
-        terms = [gram[i * stations : (i + 1) * stations] for i in range(SUB)]
-        width = tiles * LANES
+    lag_lane = lax.broadcasted_iota(jnp.int32, (stations, LANES), 1)
+
+    def one_station(a, slot_of):
+        whole = series[a]
+        pieces = []
+        for c in range(parts):
+            shift = LANES - SUB * c - 1
+            turned[slot_of, c] = pltpu.roll(whole, shift, 1)
+            moved = [turned[slot_of, c, v : v + nk] for v in range(tiles + 1)]
+            pieces.append(
+                jnp.concatenate(
+                    [jnp.where(lane < shift, moved[v], moved[v + 1]) for v in range(tiles)], axis=1
+                ).astype(jnp.bfloat16)
+            )
+        gram = jnp.dot(lhs, jnp.concatenate(pieces, axis=0), preferred_element_type=jnp.float32)
+        back = (LANES - SUB * (a % per_tile)) % LANES
+        terms = []
+        for i in range(SUB):
+            term = gram[i * stations : (i + 1) * stations]
+            if i:
+                tail = tails[a // per_tile, i * stations : (i + 1) * stations]
+                head = jnp.where(lag_lane < i, pltpu.roll(tail, back, 1), term[:, :LANES])
+                term = jnp.concatenate([head, term[:, LANES:]], axis=1)
+            terms.append(term)
         step = 1
         while len(terms) > 1:
             terms = [
-                terms[i] + pltpu.roll(terms[i + 1], width - step, 1)
+                terms[i] + pltpu.roll(terms[i + 1], LAGS - step, 1)
                 for i in range(0, len(terms), 2)
             ]
             step *= 2
-        total = pltpu.roll(terms[0], width - 1, 1)[:, :LAGS] * scale
-        sums[a] = jnp.dot(
-            select, total.astype(jnp.bfloat16), preferred_element_type=jnp.float32
-        ).astype(jnp.bfloat16)[:rows]
+        total = (terms[0] * scale).astype(jnp.bfloat16)
+        sums[a] = jnp.dot(select, total, preferred_element_type=jnp.float32)[:rows]
+
+    def pair(step, carry):
+        one_station(2 * step, 0)
+        one_station(2 * step + 1, 1)
+        return carry
+
+    lax.fori_loop(0, own_count // 2, pair, 0)
     for a in range(own_count):
-        out[:, a, :] = jnp.dot(
-            sums[a], flip[...], preferred_element_type=jnp.float32
-        ).astype(jnp.bfloat16)
+        order[:, a, :] = sums[a]
+    square = (LAGS, LAGS)
+    ends = lax.broadcasted_iota(jnp.int32, square, 0) + lax.broadcasted_iota(jnp.int32, square, 1)
+    flip = jnp.where(ends == LAGS - 1, 1.0, 0.0).astype(jnp.bfloat16)
+    out[...] = (
+        jnp.dot(
+            order[...].reshape(rows * own_count, LAGS).astype(jnp.bfloat16),
+            flip,
+            preferred_element_type=jnp.float32,
+        )
+        .astype(jnp.bfloat16)
+        .reshape(rows, own_count, LAGS)
+    )
 
 
 def on_device(n_sta, n_seg, records, owners):
@@ -399,10 +452,9 @@
     nk = n1 * n_seg
     blocks = own_count // BS
     slots = max(2, 2 * blocks * DESTS // n_sta)
-    names = jnp.pad(
-        owners.astype(jnp.bfloat16), ((0, own_count - blocks), (0, LANES - DESTS))
-    )
     vmem = pl.BlockSpec(memory_space=pltpu.VMEM)
+    hbm = pl.BlockSpec(memory_space=pltpu.HBM)
+    constants = tables(seg_len)
     white, own, received = pl.pallas_call(
         functools.partial(gather_kernel, n_sta, n_seg),
         out_shape=(
@@ -410,10 +462,13 @@
             jax.ShapeDtypeStruct((nk + 1, own_count, LANES), jnp.bfloat16),
             jax.ShapeDtypeStruct((depth, nk + 1, own_count, LANES), jnp.bfloat16),
         ),
-        in_specs=[vmem] * 5,
+        in_specs=[hbm, vmem, hbm, hbm, hbm],
         out_specs=(vmem,) * 3,
         scratch_shapes=[
             pltpu.VMEM((n_seg, own_count, seg_len), jnp.bfloat16),
+            *(pltpu.VMEM(table.shape, table.dtype) for table in constants),
+            pltpu.VMEM((own_count, LANES), jnp.float32),
+            pltpu.SemaphoreType.DMA((1 + len(constants),)),
             pltpu.SemaphoreType.DMA((n_seg - 1,)),
             pltpu.SemaphoreType.DMA((n_seg - 1,)),
             pltpu.SemaphoreType.DMA((2 * n_seg,)),
@@ -425,26 +480,29 @@
             collective_id=0, has_side_effects=True, vmem_limit_bytes=32 * 2**20
         ),
         name="whiten_and_gather",
-    )(records, names, *tables(seg_len))
+    )(records, owners.T, *constants)
     stations = depth * own_count
     rows = depth * slots * BS
-    flip = jnp.asarray(np.eye(LAGS)[::-1], jnp.bfloat16)
     parts = LANES // SUB
-    tiles = LAGS // LANES + 1
+    length = (nk + LAGS // LANES + 1 + 7) // 8 * 8
     correlations = pl.pallas_call(
         functools.partial(lag_kernel, n_sta, n_seg, slots),
         out_shape=jax.ShapeDtypeStruct((rows, own_count, LAGS), jnp.bfloat16),
-        in_specs=[vmem] * 3,
+        in_specs=[vmem] * 2,
         out_specs=vmem,
         scratch_shapes=[
-            pltpu.VMEM((parts, nk + tiles - 1, own_count, LANES), jnp.float32),
+            pltpu.VMEM((nk, own_count, LANES), jnp.float32),
+            pltpu.VMEM((own_count, length, LANES), jnp.float32),
+            pltpu.VMEM((2, parts, length, LANES), jnp.float32),
             pltpu.VMEM((nk, own_count, LANES), jnp.float32),
             pltpu.VMEM((SUB, stations, parts * nk), jnp.float32),
-            pltpu.VMEM((own_count, rows, LAGS), jnp.bfloat16),
+            pltpu.VMEM((own_count * SUB // LANES, SUB * stations, LANES), jnp.float32),
+            pltpu.VMEM((own_count, rows, LAGS), jnp.float32),
+            pltpu.VMEM((rows, own_count, LAGS), jnp.float32),
         ],
         compiler_params=pltpu.CompilerParams(vmem_limit_bytes=48 * 2**20),
         name="correlate",
-    )(own, received, flip)
+    )(own, received)
     return white, correlations
 
 

time: 61.4 us -> 46.7 us (0.76)
  Pallas kernels: 54.6 us -> 41.1 us
  other arithmetic: 0.69 us -> 0 us
    pallas_call x1, Pallas kernels: 31.7 us -> 17.7 us  [on_device(): pl.pallas_call(functools.partial(lag_kernel, n_sta, n_seg, slots), out_sh...]
    convert_element_type x1 -> x0, other arithmetic: 0.69 us -> none  [on_device(): owners.astype(jnp.bfloat16)]
where the time goes in v2:
time: 46.7 us; the launch traced here: 46.4 us
  Pallas kernels  41.1 us (88%)
  local copies, waits for them, and re-layouts  4.67 us (10%)
  between operations  0.65 us (1%)
    pallas_call x1, Pallas kernels, on_device(): pl.pallas_call(functools.partial(gather_kernel, n_sta, n_seg), out_shape=...  23.5 us
    pallas_call x1, Pallas kernels, on_device(): pl.pallas_call(functools.partial(lag_kernel, n_sta, n_seg, slots), out_sh...  17.7 us
    unnamed x11, local copies, waits for them, and re-layouts  4.67 us

profile of v2, /device:TPU:3, one launch (start us, length us, event | category | flops | bytes accessed | tf_op | source)
XLA Modules:
  0.0 46.4 jit_solution(12305831523356142407)
XLA Ops:
  0.6 0.0 copy-start
  0.6 0.9 %copy-done = bf16[256,256]{1,0:T(8,128)(2,1)S(1)} copy-done((bf16[256,256]{1,0:T(8,128)(2,1)S(1)}, bf16[256,256]{1,0:T(8,128)(2,1)}, u32[]{:S(2)}) %copy-start) | copy-done | bytes 131096
  1.5 0.0 copy-start.1
  1.5 0.9 %copy-done.1 = bf16[256,256]{1,0:T(8,128)(2,1)S(1)} copy-done((bf16[256,256]{1,0:T(8,128)(2,1)S(1)}, bf16[256,256]{1,0:T(8,128)(2,1)}, u32[]{:S(2)}) %copy-start.1) | copy-done | bytes 131096
  2.4 0.0 copy-start.2
  2.4 0.8 %copy-done.2 = bf16[16,2048]{1,0:T(8,128)(2,1)S(1)} copy-done((bf16[16,2048]{1,0:T(8,128)(2,1)S(1)}, bf16[16,2048]{1,0:T(8,128)(2,1)}, u32[]{:S(2)}) %copy-start.2) | copy-done | bytes 65560
  3.3 0.0 copy-start.3
  3.3 0.7 %copy-done.3 = f32[2,9,128]{2,1,0:T(8,128)S(1)} copy-done((f32[2,9,128]{2,1,0:T(8,128)S(1)}, f32[2,9,128]{2,1,0:T(8,128)}, u32[]{:S(2)}) %copy-start.3) | copy-done | bytes 9240
  4.0 0.0 copy-start.4
  4.0 0.7 %copy-done.4 = s32[8,4]{0,1:T(4,128)S(1)} copy-done((s32[8,4]{0,1:T(4,128)S(1)}, s32[8,4]{0,1:T(4,128)}, u32[]{:S(2)}) %copy-start.4) | copy-done | bytes 152
  4.7 23.5 %whiten_and_gather.1 = (bf16[16,2048]{1,0:T(8,128)(2,1)S(1)}, bf16[65,16,128]{2,1,0:T(8,128)(2,1)S(1)}, bf16[2,65,16,128]{3,2,1,0:T(8,128)(2,1)S(1)}) custom-call(bf16[16,2048]{1,0:T(8,128)(2,1)S(1)} %copy-done.2, s32[4,8]{1,0:T(4,128)S(1)} %bitcast.1, f32[2,9,128]{2,1,0:T(8,128)S(1)} %copy-done.3, bf16[256,256]{1,0:T(8,128)(2,1)S(1)} %copy-done.1, ...), custom_call_target="tpu_custom_call" | custom-call | tf_op jit(solution)/shard_map/whiten_and_gather/pallas_call | solution.py:458
  28.1 17.7 %correlate.1 = bf16[32,16,512]{2,1,0:T(8,128)(2,1)} custom-call(bf16[65,16,128]{2,1,0:T(8,128)(2,1)S(1)} %get-tuple-element.6.own, bf16[2,65,16,128]{3,2,1,0:T(8,128)(2,1)S(1)} %get-tuple-element.7.received), custom_call_target="tpu_custom_call" | custom-call | tf_op jit(solution)/shard_map/correlate/pallas_call | solution.py:488
  45.8 0.6 %copy.8 = bf16[16,2048]{1,0:T(8,128)(2,1)} copy(bf16[16,2048]{1,0:T(8,128)(2,1)S(1)} %get-tuple-element.10) | data formatting | bytes 131072
Async XLA Ops:
  0.6 0.9 %copy-start = (bf16[256,256]{1,0:T(8,128)(2,1)S(1)}, bf16[256,256]{1,0:T(8,128)(2,1)}, u32[]{:S(2)}) copy-start(bf16[256,256]{1,0:T(8,128)(2,1)} %constant.8.clone.backward_in) | copy-start | bytes 393220
  1.5 0.9 %copy-start.1 = (bf16[256,256]{1,0:T(8,128)(2,1)S(1)}, bf16[256,256]{1,0:T(8,128)(2,1)}, u32[]{:S(2)}) copy-start(bf16[256,256]{1,0:T(8,128)(2,1)} %constant.7.clone.forward_in) | copy-start | bytes 393220
  2.4 0.8 %copy-start.2 = (bf16[16,2048]{1,0:T(8,128)(2,1)S(1)}, bf16[16,2048]{1,0:T(8,128)(2,1)}, u32[]{:S(2)}) copy-start(bf16[16,2048]{1,0:T(8,128)(2,1)} %records.1) | copy-start | bytes 196612
  3.3 0.7 %copy-start.3 = (f32[2,9,128]{2,1,0:T(8,128)S(1)}, f32[2,9,128]{2,1,0:T(8,128)}, u32[]{:S(2)}) copy-start(f32[2,9,128]{2,1,0:T(8,128)} %constant.6.clone.twiddle_in) | copy-start | bytes 27652
  4.0 0.7 %copy-start.4 = (s32[8,4]{0,1:T(4,128)S(1)}, s32[8,4]{0,1:T(4,128)}, u32[]{:S(2)}) copy-start(s32[8,4]{0,1:T(4,128)} %param.6) | copy-start | bytes 388

commit v3 on v2

--- a/solution.py
+++ b/solution.py
@@ -3,7 +3,6 @@
 
 import jax
 import jax.numpy as jnp
-import numpy as np
 from jax import lax
 from jax.experimental import pallas as pl
 from jax.experimental.pallas import tpu as pltpu
@@ -73,22 +72,23 @@
     return slabs
 
 
-def tables(seg_len):
-    lanes = np.arange(LANES)
-    angle = 2 * np.pi * (np.outer(lanes, lanes) % LANES) / LANES
-    c, s = np.cos(angle), np.sin(angle)
-    forward = np.block([[c, s], [-s, c]])
-    count = seg_len // LANES // 2 + 1
-    turn = 2 * np.pi * np.outer(np.arange(count), lanes) / seg_len
-    twiddle = np.stack([np.cos(turn), np.sin(turn)]).astype(np.float32)
-    return (
-        jnp.asarray(twiddle),
-        jnp.asarray(forward, jnp.bfloat16),
-        jnp.asarray(forward.T, jnp.bfloat16),
+def make_tables(seg_len, count):
+    shape = (LANES, LANES)
+    row = lax.broadcasted_iota(jnp.int32, shape, 0)
+    lane = lax.broadcasted_iota(jnp.int32, shape, 1)
+    angle = (row * lane % LANES).astype(jnp.float32) * (2 * math.pi / LANES)
+    c, s = jnp.cos(angle).astype(jnp.bfloat16), jnp.sin(angle).astype(jnp.bfloat16)
+    forward = jnp.concatenate(
+        [jnp.concatenate([c, s], axis=1), jnp.concatenate([-s, c], axis=1)], axis=0
     )
-
-
-def whiten(slabs, seg_count, own_count, twiddle, forward, backward):
+    backward = jnp.concatenate(
+        [jnp.concatenate([c, -s], axis=1), jnp.concatenate([s, c], axis=1)], axis=0
+    )
+    turn = (row * lane)[:count].astype(jnp.float32) * (2 * math.pi / seg_len)
+    return jnp.cos(turn), jnp.sin(turn), forward, backward
+
+
+def whiten(slabs, seg_count, own_count, cosine, sine, forward, backward):
     n1 = len(slabs)
     seg_len = n1 * LANES
     window = seg_len * seg_count
@@ -107,7 +107,7 @@
     turned = []
     for k, (re, im) in enumerate(first):
         if k:
-            c, s = twiddle[0, k : k + 1, :], twiddle[1, k : k + 1, :]
+            c, s = cosine[k : k + 1], sine[k : k + 1]
             re, im = re * c - im * s, re * s + im * c
         turned.append(jnp.concatenate([re, im], axis=1).astype(jnp.bfloat16))
     spectrum = jnp.dot(
@@ -134,7 +134,7 @@
         re = back[k * rows : (k + 1) * rows, :LANES]
         im = back[k * rows : (k + 1) * rows, LANES:]
         if k:
-            c, s = twiddle[0, k : k + 1, :], twiddle[1, k : k + 1, :]
+            c, s = cosine[k : k + 1], sine[k : k + 1]
             re, im = re * c + im * s, im * c - re * s
         turned.append((re, im))
     trace = [slab * (1.0 / seg_len) for slab in real_inverse(turned, n1)]
@@ -150,18 +150,10 @@
     n_seg,
     records,
     owners,
-    twiddle_in,
-    forward_in,
-    backward_in,
-    white,
     own,
     received,
     held,
-    twiddle,
-    forward,
-    backward,
     names,
-    table_sem,
     seg_send,
     seg_recv,
     z_send,
@@ -176,19 +168,6 @@
     g, s = lax.axis_index("seg"), lax.axis_index("sta")
     z, y = s // depth, s % depth
 
-    fetches = [
-        pltpu.make_async_copy(source, target, table_sem.at[i])
-        for i, (source, target) in enumerate(
-            (
-                (records, held.at[g]),
-                (twiddle_in, twiddle),
-                (forward_in, forward),
-                (backward_in, backward),
-            )
-        )
-    ]
-    for fetch in fetches:
-        fetch.start()
     names[...] = jnp.zeros_like(names)
     names[: owners.shape[0], : owners.shape[1]] = owners[...].astype(jnp.float32)
     barrier = pltpu.get_barrier_semaphore()
@@ -222,8 +201,8 @@
         )
         copy.start()
         copies.append(copy)
-    for fetch in fetches:
-        fetch.wait()
+    held[g] = records[...]
+    made = make_tables(seg_len, (n1 // 2 + 8) // 8 * 8)
     for copy in copies:
         copy.wait()
 
@@ -235,7 +214,7 @@
                 axis=0,
             )
         )
-    result = whiten(slabs, n_seg, own_count, twiddle, forward[...], backward[...])
+    result = whiten(slabs, n_seg, own_count, *made)
     for t in range(n1):
         rounded = result[t].astype(jnp.bfloat16)
         for j in range(n_seg):
@@ -304,8 +283,6 @@
 
         for d in range(1, depth):
             along_y(j, d).start()
-    for t in range(n1):
-        white[:, t * LANES : (t + 1) * LANES] = own[g * n1 + t]
     for j in range(n_seg):
         for d in range(1, depth):
             along_y(j, d).wait()
@@ -319,7 +296,7 @@
             along_z_down(j).wait_send()
 
 
-def lag_kernel(n_sta, n_seg, slots, own, received, out, flat, series, turned, rec, left, tails, sums, order):
+def lag_kernel(n_sta, n_seg, slots, own, received, white, out, flat, series, turned, shifted, rec, left, tails, grams, sums, order):
     depth = n_sta // n_seg
     nk, own_count = own.shape[0] - 1, own.shape[1]
     stations = depth * own_count
@@ -328,6 +305,12 @@
     edge = LAGS // 2 // LANES
     per_tile = LANES // SUB
     me = lax.axis_index("sta").astype(jnp.float32)
+    length = series.shape[1]
+
+    g = lax.axis_index("seg")
+    n1 = nk // n_seg
+    for t in range(n1):
+        white[:, t * LANES : (t + 1) * LANES] = own[g * n1 + t]
 
     flat[...] = own[:nk].astype(jnp.float32)
     series[...] = jnp.zeros_like(series)
@@ -354,11 +337,17 @@
                 moved = pltpu.roll(moved, shift, 1) if shift else moved
                 piece = jnp.where(lane // SUB == q, moved, piece)
             pieces.append(piece)
-        tails[first // per_tile] = jnp.dot(
+        ends_of = jnp.dot(
             lhs,
             jnp.concatenate(pieces, axis=0).astype(jnp.bfloat16),
             preferred_element_type=jnp.float32,
         )
+        place = lax.broadcasted_iota(jnp.int32, (stations, LANES), 1)
+        added = jnp.zeros((stations, LANES), jnp.float32)
+        for i in range(1, SUB):
+            part = jnp.where(place % SUB < i, ends_of[i * stations : (i + 1) * stations], 0.0)
+            added += pltpu.roll(part, SUB - i, 1)
+        tails[first // per_tile] = added
 
     shape = (stations, stations)
     row = lax.broadcasted_iota(jnp.int32, shape, 0)
@@ -389,39 +378,45 @@
     rows = out.shape[0]
     window = nk * LANES
     scale = 1.0 / math.sqrt(window)
-    lag_lane = lax.broadcasted_iota(jnp.int32, (stations, LANES), 1)
-
-    def one_station(a, slot_of):
+    last = lax.broadcasted_iota(jnp.int32, (stations, LANES), 1) >= LANES - SUB
+    across_lanes = lax.broadcasted_iota(jnp.int32, (8, LAGS), 1)
+    whole_lane = lax.broadcasted_iota(jnp.int32, (length - 8, LANES), 1)
+
+    def one_station(a, half):
         whole = series[a]
         pieces = []
         for c in range(parts):
             shift = LANES - SUB * c - 1
-            turned[slot_of, c] = pltpu.roll(whole, shift, 1)
-            moved = [turned[slot_of, c, v : v + nk] for v in range(tiles + 1)]
+            moved = pltpu.roll(whole, shift, 1)
+            turned[half, c] = moved
+            shifted[half, c] = jnp.where(
+                whole_lane < shift, moved[: length - 8], turned[half, c, 1 : length - 7]
+            )
             pieces.append(
                 jnp.concatenate(
-                    [jnp.where(lane < shift, moved[v], moved[v + 1]) for v in range(tiles)], axis=1
+                    [shifted[half, c, v : v + nk] for v in range(tiles)], axis=1
                 ).astype(jnp.bfloat16)
             )
-        gram = jnp.dot(lhs, jnp.concatenate(pieces, axis=0), preferred_element_type=jnp.float32)
-        back = (LANES - SUB * (a % per_tile)) % LANES
-        terms = []
-        for i in range(SUB):
-            term = gram[i * stations : (i + 1) * stations]
-            if i:
-                tail = tails[a // per_tile, i * stations : (i + 1) * stations]
-                head = jnp.where(lag_lane < i, pltpu.roll(tail, back, 1), term[:, :LANES])
-                term = jnp.concatenate([head, term[:, LANES:]], axis=1)
-            terms.append(term)
-        step = 1
-        while len(terms) > 1:
-            terms = [
-                terms[i] + pltpu.roll(terms[i + 1], LAGS - step, 1)
-                for i in range(0, len(terms), 2)
-            ]
-            step *= 2
-        total = (terms[0] * scale).astype(jnp.bfloat16)
-        sums[a] = jnp.dot(select, total, preferred_element_type=jnp.float32)[:rows]
+        grams[half] = jnp.dot(
+            lhs, jnp.concatenate(pieces, axis=0), preferred_element_type=jnp.float32
+        )
+        totals = []
+        for r in range(0, stations, 8):
+            total = jnp.zeros((8, LAGS), jnp.float32)
+            for i in reversed(range(SUB)):
+                term = grams[half, i * stations + r : i * stations + r + 8]
+                if i < SUB - 1:
+                    total = pltpu.roll(total, LAGS - 1, 1)
+                total = total + (jnp.where(across_lanes < i, 0.0, term) if i else term)
+            totals.append(total)
+        total = jnp.concatenate(totals, axis=0)
+        move = (LANES - SUB - SUB * (a % per_tile)) % LANES
+        tail = pltpu.roll(tails[a // per_tile], move, 1)
+        edge_tile = total[:, LAGS - LANES :] + jnp.where(last, tail, 0.0)
+        total = jnp.concatenate([total[:, : LAGS - LANES], edge_tile], axis=1)
+        sums[a] = jnp.dot(
+            select, (total * scale).astype(jnp.bfloat16), preferred_element_type=jnp.float32
+        )[:rows]
 
     def pair(step, carry):
         one_station(2 * step, 0)
@@ -453,22 +448,17 @@
     blocks = own_count // BS
     slots = max(2, 2 * blocks * DESTS // n_sta)
     vmem = pl.BlockSpec(memory_space=pltpu.VMEM)
-    hbm = pl.BlockSpec(memory_space=pltpu.HBM)
-    constants = tables(seg_len)
-    white, own, received = pl.pallas_call(
+    own, received = pl.pallas_call(
         functools.partial(gather_kernel, n_sta, n_seg),
         out_shape=(
-            jax.ShapeDtypeStruct((own_count, seg_len), jnp.bfloat16),
             jax.ShapeDtypeStruct((nk + 1, own_count, LANES), jnp.bfloat16),
             jax.ShapeDtypeStruct((depth, nk + 1, own_count, LANES), jnp.bfloat16),
         ),
-        in_specs=[hbm, vmem, hbm, hbm, hbm],
-        out_specs=(vmem,) * 3,
+        in_specs=[vmem] * 2,
+        out_specs=(vmem,) * 2,
         scratch_shapes=[
             pltpu.VMEM((n_seg, own_count, seg_len), jnp.bfloat16),
-            *(pltpu.VMEM(table.shape, table.dtype) for table in constants),
             pltpu.VMEM((own_count, LANES), jnp.float32),
-            pltpu.SemaphoreType.DMA((1 + len(constants),)),
             pltpu.SemaphoreType.DMA((n_seg - 1,)),
             pltpu.SemaphoreType.DMA((n_seg - 1,)),
             pltpu.SemaphoreType.DMA((2 * n_seg,)),
@@ -480,23 +470,28 @@
             collective_id=0, has_side_effects=True, vmem_limit_bytes=32 * 2**20
         ),
         name="whiten_and_gather",
-    )(records, owners.T, *constants)
+    )(records, owners.T)
     stations = depth * own_count
     rows = depth * slots * BS
     parts = LANES // SUB
-    length = (nk + LAGS // LANES + 1 + 7) // 8 * 8
-    correlations = pl.pallas_call(
+    length = (nk + LAGS // LANES + 7) // 8 * 8 + 8
+    white, correlations = pl.pallas_call(
         functools.partial(lag_kernel, n_sta, n_seg, slots),
-        out_shape=jax.ShapeDtypeStruct((rows, own_count, LAGS), jnp.bfloat16),
+        out_shape=(
+            jax.ShapeDtypeStruct((own_count, seg_len), jnp.bfloat16),
+            jax.ShapeDtypeStruct((rows, own_count, LAGS), jnp.bfloat16),
+        ),
         in_specs=[vmem] * 2,
-        out_specs=vmem,
+        out_specs=(vmem,) * 2,
         scratch_shapes=[
             pltpu.VMEM((nk, own_count, LANES), jnp.float32),
             pltpu.VMEM((own_count, length, LANES), jnp.float32),
             pltpu.VMEM((2, parts, length, LANES), jnp.float32),
+            pltpu.VMEM((2, parts, length - 8, LANES), jnp.float32),
             pltpu.VMEM((nk, own_count, LANES), jnp.float32),
             pltpu.VMEM((SUB, stations, parts * nk), jnp.float32),
-            pltpu.VMEM((own_count * SUB // LANES, SUB * stations, LANES), jnp.float32),
+            pltpu.VMEM((own_count * SUB // LANES, stations, LANES), jnp.float32),
+            pltpu.VMEM((2, SUB * stations, LAGS), jnp.float32),
             pltpu.VMEM((own_count, rows, LAGS), jnp.float32),
             pltpu.VMEM((rows, own_count, LAGS), jnp.float32),
         ],

time: 46.7 us -> 55.7 us (1.19)
  Pallas kernels: 41.1 us -> 53.3 us
  local copies, waits for them, and re-layouts: 4.67 us -> 1.51 us
    pallas_call x1, Pallas kernels: 17.7 us -> 30.3 us  [on_device(): pl.pallas_call(functools.partial(lag_kernel, n_sta, n_seg, slots), out_sh...]
    unnamed x11 -> x4, local copies, waits for them, and re-layouts: 4.67 us -> 1.51 us
where the time goes in v3:
time: 55.7 us; the launch traced here: 55.5 us
  Pallas kernels  53.3 us (96%)
  local copies, waits for them, and re-layouts  1.51 us (3%)
  between operations  0.65 us (1%)
    pallas_call x1, Pallas kernels, on_device(): pl.pallas_call(functools.partial(lag_kernel, n_sta, n_seg, slots), out_sh...  30.3 us
    pallas_call x1, Pallas kernels, on_device(): pl.pallas_call(functools.partial(gather_kernel, n_sta, n_seg), out_shape=...  23 us
    unnamed x4, local copies, waits for them, and re-layouts  1.51 us

profile of v3, /device:TPU:3, one launch (start us, length us, event | category | flops | bytes accessed | tf_op | source)
XLA Modules:
  0.0 55.5 jit_solution(17511735264209713286)
XLA Ops:
  0.6 0.0 copy-start
  0.6 0.8 %copy-done = bf16[16,2048]{1,0:T(8,128)(2,1)S(1)} copy-done((bf16[16,2048]{1,0:T(8,128)(2,1)S(1)}, bf16[16,2048]{1,0:T(8,128)(2,1)}, u32[]{:S(2)}) %copy-start) | copy-done | bytes 65560
  1.5 0.0 copy-start.1
  1.5 0.7 %copy-done.1 = s32[8,4]{0,1:T(4,128)S(1)} copy-done((s32[8,4]{0,1:T(4,128)S(1)}, s32[8,4]{0,1:T(4,128)}, u32[]{:S(2)}) %copy-start.1) | copy-done | bytes 152
  2.2 23.0 %whiten_and_gather.1 = (bf16[65,16,128]{2,1,0:T(8,128)(2,1)S(1)}, bf16[2,65,16,128]{3,2,1,0:T(8,128)(2,1)S(1)}) custom-call(bf16[16,2048]{1,0:T(8,128)(2,1)S(1)} %copy-done, s32[4,8]{1,0:T(4,128)S(1)} %bitcast.1), custom_call_target="tpu_custom_call" | custom-call | tf_op jit(solution)/shard_map/whiten_and_gather/pallas_call | solution.py:451
  25.1 30.3 %correlate.1 = (bf16[16,2048]{1,0:T(8,128)(2,1)}, bf16[32,16,512]{2,1,0:T(8,128)(2,1)}) custom-call(bf16[65,16,128]{2,1,0:T(8,128)(2,1)S(1)} %get-tuple-element.4.own, bf16[2,65,16,128]{3,2,1,0:T(8,128)(2,1)S(1)} %get-tuple-element.5.received), custom_call_target="tpu_custom_call" | custom-call | tf_op jit(solution)/shard_map/correlate/pallas_call | solution.py:478
Async XLA Ops:
  0.6 0.8 %copy-start = (bf16[16,2048]{1,0:T(8,128)(2,1)S(1)}, bf16[16,2048]{1,0:T(8,128)(2,1)}, u32[]{:S(2)}) copy-start(bf16[16,2048]{1,0:T(8,128)(2,1)} %records.1) | copy-start | bytes 196612
  1.5 0.7 %copy-start.1 = (s32[8,4]{0,1:T(4,128)S(1)}, s32[8,4]{0,1:T(4,128)}, u32[]{:S(2)}) copy-start(s32[8,4]{0,1:T(4,128)} %param.3) | copy-start | bytes 388

commit v4 on v3

--- a/solution.py
+++ b/solution.py
@@ -151,9 +151,11 @@
     records,
     owners,
     own,
+    series,
     received,
     held,
     names,
+    flat,
     seg_send,
     seg_recv,
     z_send,
@@ -219,6 +221,7 @@
         rounded = result[t].astype(jnp.bfloat16)
         for j in range(n_seg):
             own[j * n1 + t] = rounded[j * own_count : (j + 1) * own_count]
+            flat[j * n1 + t] = rounded[j * own_count : (j + 1) * own_count].astype(jnp.float32)
     own[n_seg * n1] = names[...].astype(jnp.bfloat16)
 
     @pl.when(z == g)
@@ -267,12 +270,7 @@
             device_id_type=MESH,
         )
 
-    for j in range(n_seg):
-
-        @pl.when(z != g)
-        def _():
-            along_z_up(j).wait_recv()
-
+    def send(j):
         @pl.when(up)
         def _():
             along_z_up(j).start()
@@ -283,6 +281,23 @@
 
         for d in range(1, depth):
             along_y(j, d).start()
+
+    @pl.when(z == g)
+    def _():
+        for j in range(n_seg):
+            send(j)
+
+    edge = LAGS // 2 // LANES
+    series[...] = jnp.zeros_like(series)
+    for a in range(own_count):
+        series[a, edge : edge + n_seg * n1] = flat[:, a, :]
+
+    @pl.when(z != g)
+    def _():
+        for j in range(n_seg):
+            along_z_up(j).wait_recv()
+            send(j)
+
     for j in range(n_seg):
         for d in range(1, depth):
             along_y(j, d).wait()
@@ -296,13 +311,12 @@
             along_z_down(j).wait_send()
 
 
-def lag_kernel(n_sta, n_seg, slots, own, received, white, out, flat, series, turned, shifted, rec, left, tails, grams, sums, order):
+def lag_kernel(n_sta, n_seg, slots, own, series, received, white, out, turned, shifted, rec, left, tails, grams, sums, order):
     depth = n_sta // n_seg
     nk, own_count = own.shape[0] - 1, own.shape[1]
     stations = depth * own_count
     parts = LANES // SUB
     tiles = LAGS // LANES
-    edge = LAGS // 2 // LANES
     per_tile = LANES // SUB
     me = lax.axis_index("sta").astype(jnp.float32)
     length = series.shape[1]
@@ -311,11 +325,6 @@
     n1 = nk // n_seg
     for t in range(n1):
         white[:, t * LANES : (t + 1) * LANES] = own[g * n1 + t]
-
-    flat[...] = own[:nk].astype(jnp.float32)
-    series[...] = jnp.zeros_like(series)
-    for a in range(own_count):
-        series[a, edge : edge + nk] = flat[:, a, :]
 
     for y in range(depth):
         rec[...] = received[y, :nk].astype(jnp.float32)
@@ -378,8 +387,8 @@
     rows = out.shape[0]
     window = nk * LANES
     scale = 1.0 / math.sqrt(window)
-    last = lax.broadcasted_iota(jnp.int32, (stations, LANES), 1) >= LANES - SUB
-    across_lanes = lax.broadcasted_iota(jnp.int32, (8, LAGS), 1)
+    lag_lane = lax.broadcasted_iota(jnp.int32, (stations, LANES), 1)
+    last = lag_lane >= LANES - SUB
     whole_lane = lax.broadcasted_iota(jnp.int32, (length - 8, LANES), 1)
 
     def one_station(a, half):
@@ -400,16 +409,17 @@
         grams[half] = jnp.dot(
             lhs, jnp.concatenate(pieces, axis=0), preferred_element_type=jnp.float32
         )
-        totals = []
-        for r in range(0, stations, 8):
-            total = jnp.zeros((8, LAGS), jnp.float32)
-            for i in reversed(range(SUB)):
-                term = grams[half, i * stations + r : i * stations + r + 8]
-                if i < SUB - 1:
-                    total = pltpu.roll(total, LAGS - 1, 1)
-                total = total + (jnp.where(across_lanes < i, 0.0, term) if i else term)
-            totals.append(total)
-        total = jnp.concatenate(totals, axis=0)
+
+        def diagonal(first, count):
+            if count == 1:
+                term = grams[half, first * stations : (first + 1) * stations]
+                head = jnp.where(lag_lane < first, 0.0, term[:, :LANES])
+                return jnp.concatenate([head, term[:, LANES:]], axis=1) if first else term
+            count //= 2
+            later = pltpu.roll(diagonal(first + count, count), LAGS - count, 1)
+            return diagonal(first, count) + later
+
+        total = diagonal(0, SUB)
         move = (LANES - SUB - SUB * (a % per_tile)) % LANES
         tail = pltpu.roll(tails[a // per_tile], move, 1)
         edge_tile = total[:, LAGS - LANES :] + jnp.where(last, tail, 0.0)
@@ -445,20 +455,23 @@
     depth = n_sta // n_seg
     n1 = seg_len // LANES
     nk = n1 * n_seg
+    length = (nk + LAGS // LANES + 7) // 8 * 8 + 8
     blocks = own_count // BS
     slots = max(2, 2 * blocks * DESTS // n_sta)
     vmem = pl.BlockSpec(memory_space=pltpu.VMEM)
-    own, received = pl.pallas_call(
+    own, series, received = pl.pallas_call(
         functools.partial(gather_kernel, n_sta, n_seg),
         out_shape=(
             jax.ShapeDtypeStruct((nk + 1, own_count, LANES), jnp.bfloat16),
+            jax.ShapeDtypeStruct((own_count, length, LANES), jnp.float32),
             jax.ShapeDtypeStruct((depth, nk + 1, own_count, LANES), jnp.bfloat16),
         ),
         in_specs=[vmem] * 2,
-        out_specs=(vmem,) * 2,
+        out_specs=(vmem,) * 3,
         scratch_shapes=[
             pltpu.VMEM((n_seg, own_count, seg_len), jnp.bfloat16),
             pltpu.VMEM((own_count, LANES), jnp.float32),
+            pltpu.VMEM((nk, own_count, LANES), jnp.float32),
             pltpu.SemaphoreType.DMA((n_seg - 1,)),
             pltpu.SemaphoreType.DMA((n_seg - 1,)),
             pltpu.SemaphoreType.DMA((2 * n_seg,)),
@@ -474,18 +487,15 @@
     stations = depth * own_count
     rows = depth * slots * BS
     parts = LANES // SUB
-    length = (nk + LAGS // LANES + 7) // 8 * 8 + 8
     white, correlations = pl.pallas_call(
         functools.partial(lag_kernel, n_sta, n_seg, slots),
         out_shape=(
             jax.ShapeDtypeStruct((own_count, seg_len), jnp.bfloat16),
             jax.ShapeDtypeStruct((rows, own_count, LAGS), jnp.bfloat16),
         ),
-        in_specs=[vmem] * 2,
+        in_specs=[vmem] * 3,
         out_specs=(vmem,) * 2,
         scratch_shapes=[
-            pltpu.VMEM((nk, own_count, LANES), jnp.float32),
-            pltpu.VMEM((own_count, length, LANES), jnp.float32),
             pltpu.VMEM((2, parts, length, LANES), jnp.float32),
             pltpu.VMEM((2, parts, length - 8, LANES), jnp.float32),
             pltpu.VMEM((nk, own_count, LANES), jnp.float32),
@@ -497,7 +507,7 @@
         ],
         compiler_params=pltpu.CompilerParams(vmem_limit_bytes=48 * 2**20),
         name="correlate",
-    )(own, received)
+    )(own, series, received)
     return white, correlations
 
 

time: 55.7 us -> 43.3 us (0.78)
  Pallas kernels: 53.3 us -> 41 us
    pallas_call x1, Pallas kernels: 30.3 us -> 18 us  [on_device(): pl.pallas_call(functools.partial(lag_kernel, n_sta, n_seg, slots), out_sh...]
where the time goes in v4:
time: 43.3 us; the launch traced here: 43.1 us
  Pallas kernels  41 us (95%)
  local copies, waits for them, and re-layouts  1.51 us (3%)
  between operations  0.65 us (2%)
    pallas_call x1, Pallas kernels, on_device(): pl.pallas_call(functools.partial(gather_kernel, n_sta, n_seg), out_shape=...  23 us
    pallas_call x1, Pallas kernels, on_device(): pl.pallas_call(functools.partial(lag_kernel, n_sta, n_seg, slots), out_sh...  18 us
    unnamed x4, local copies, waits for them, and re-layouts  1.51 us

profile of v4, /device:TPU:3, one launch (start us, length us, event | category | flops | bytes accessed | tf_op | source)
XLA Modules:
  0.0 43.1 jit_solution(3525749723573183025)
XLA Ops:
  0.6 0.0 copy-start
  0.6 0.8 %copy-done = bf16[16,2048]{1,0:T(8,128)(2,1)S(1)} copy-done((bf16[16,2048]{1,0:T(8,128)(2,1)S(1)}, bf16[16,2048]{1,0:T(8,128)(2,1)}, u32[]{:S(2)}) %copy-start) | copy-done | bytes 65560
  1.5 0.0 copy-start.1
  1.5 0.7 %copy-done.1 = s32[8,4]{0,1:T(4,128)S(1)} copy-done((s32[8,4]{0,1:T(4,128)S(1)}, s32[8,4]{0,1:T(4,128)}, u32[]{:S(2)}) %copy-start.1) | copy-done | bytes 152
  2.2 23.0 %whiten_and_gather.1 = (bf16[65,16,128]{2,1,0:T(8,128)(2,1)S(1)}, f32[16,80,128]{2,1,0:T(8,128)S(1)}, bf16[2,65,16,128]{3,2,1,0:T(8,128)(2,1)S(1)}) custom-call(bf16[16,2048]{1,0:T(8,128)(2,1)S(1)} %copy-done, s32[4,8]{1,0:T(4,128)S(1)} %bitcast.1), custom_call_target="tpu_custom_call" | custom-call | tf_op jit(solution)/shard_map/whiten_and_gather/pallas_call | solution.py:462
  25.2 18.0 %correlate.1 = (bf16[16,2048]{1,0:T(8,128)(2,1)}, bf16[32,16,512]{2,1,0:T(8,128)(2,1)}) custom-call(bf16[65,16,128]{2,1,0:T(8,128)(2,1)S(1)} %get-tuple-element.5.own, f32[16,80,128]{2,1,0:T(8,128)S(1)} %get-tuple-element.6.series, bf16[2,65,16,128]{3,2,1,0:T(8,128)(2,1)S(1)} %get-tuple-element.7.received), custom_call_target="tpu_custom_call" | custom-call | tf_op jit(solution)/shard_map/correlate/pallas_call | solution.py:490
Async XLA Ops:
  0.6 0.8 %copy-start = (bf16[16,2048]{1,0:T(8,128)(2,1)S(1)}, bf16[16,2048]{1,0:T(8,128)(2,1)}, u32[]{:S(2)}) copy-start(bf16[16,2048]{1,0:T(8,128)(2,1)} %records.1) | copy-start | bytes 196612
  1.5 0.7 %copy-start.1 = (s32[8,4]{0,1:T(4,128)S(1)}, s32[8,4]{0,1:T(4,128)}, u32[]{:S(2)}) copy-start(s32[8,4]{0,1:T(4,128)} %param.3) | copy-start | bytes 388

commit v5 on v4

--- a/solution.py
+++ b/solution.py
@@ -311,7 +311,7 @@
             along_z_down(j).wait_send()
 
 
-def lag_kernel(n_sta, n_seg, slots, own, series, received, white, out, turned, shifted, rec, left, tails, grams, sums, order):
+def lag_kernel(n_sta, n_seg, slots, own, series, received, white, out, turned, shifted, rhs, rec, left, lhs, tails, grams, sums, order):
     depth = n_sta // n_seg
     nk, own_count = own.shape[0] - 1, own.shape[1]
     stations = depth * own_count
@@ -333,7 +333,7 @@
             left[:, y * own_count + b, :] = jnp.concatenate(
                 [across[c * SUB : (c + 1) * SUB] for c in range(parts)], axis=1
             )
-    lhs = left[...].reshape(SUB * stations, parts * nk).astype(jnp.bfloat16)
+    lhs[...] = left[...].reshape(SUB * stations, parts * nk).astype(jnp.bfloat16)
 
     lane = lax.broadcasted_iota(jnp.int32, (nk, LANES), 1)
     for first in range(0, own_count, per_tile):
@@ -347,7 +347,7 @@
                 piece = jnp.where(lane // SUB == q, moved, piece)
             pieces.append(piece)
         ends_of = jnp.dot(
-            lhs,
+            lhs[...],
             jnp.concatenate(pieces, axis=0).astype(jnp.bfloat16),
             preferred_element_type=jnp.float32,
         )
@@ -391,49 +391,65 @@
     last = lag_lane >= LANES - SUB
     whole_lane = lax.broadcasted_iota(jnp.int32, (length - 8, LANES), 1)
 
-    def one_station(a, half):
+    def build(a, half, phases):
         whole = series[a]
-        pieces = []
-        for c in range(parts):
+        for c in phases:
             shift = LANES - SUB * c - 1
             moved = pltpu.roll(whole, shift, 1)
             turned[half, c] = moved
             shifted[half, c] = jnp.where(
                 whole_lane < shift, moved[: length - 8], turned[half, c, 1 : length - 7]
             )
-            pieces.append(
-                jnp.concatenate(
-                    [shifted[half, c, v : v + nk] for v in range(tiles)], axis=1
-                ).astype(jnp.bfloat16)
-            )
-        grams[half] = jnp.dot(
-            lhs, jnp.concatenate(pieces, axis=0), preferred_element_type=jnp.float32
-        )
-
-        def diagonal(first, count):
-            if count == 1:
-                term = grams[half, first * stations : (first + 1) * stations]
-                head = jnp.where(lag_lane < first, 0.0, term[:, :LANES])
-                return jnp.concatenate([head, term[:, LANES:]], axis=1) if first else term
-            count //= 2
-            later = pltpu.roll(diagonal(first + count, count), LAGS - count, 1)
-            return diagonal(first, count) + later
-
-        total = diagonal(0, SUB)
+            for v in range(tiles):
+                rhs[half, c * nk : (c + 1) * nk, v * LANES : (v + 1) * LANES] = shifted[
+                    half, c, v : v + nk
+                ].astype(jnp.bfloat16)
+
+    def diagonal(half, low, size, first, count):
+        if count == 1:
+            start = first * stations + low
+            term = grams[half, start : start + size]
+            if not first:
+                return term
+            head = jnp.where(lag_lane[:size] < first, 0.0, term[:, :LANES])
+            return jnp.concatenate([head, term[:, LANES:]], axis=1)
+        count //= 2
+        later = pltpu.roll(
+            diagonal(half, low, size, first + count, count), LAGS - count, 1
+        )
+        return diagonal(half, low, size, first, count) + later
+
+    def finish(a, slot_of, total):
         move = (LANES - SUB - SUB * (a % per_tile)) % LANES
         tail = pltpu.roll(tails[a // per_tile], move, 1)
         edge_tile = total[:, LAGS - LANES :] + jnp.where(last, tail, 0.0)
         total = jnp.concatenate([total[:, : LAGS - LANES], edge_tile], axis=1)
-        sums[a] = jnp.dot(
+        sums[slot_of] = jnp.dot(
             select, (total * scale).astype(jnp.bfloat16), preferred_element_type=jnp.float32
         )[:rows]
 
+    def one_step(a, half):
+        other, following = 1 - half, jnp.minimum(a + 1, own_count - 1)
+        previous = (a + own_count - 1) % own_count
+        halves = []
+        for n in range(2):
+            columns = slice(n * LAGS // 2, (n + 1) * LAGS // 2)
+            grams[half, :, columns] = jnp.dot(
+                lhs[...], rhs[half, :, columns], preferred_element_type=jnp.float32
+            )
+            build(following, other, range(n * parts // 2, (n + 1) * parts // 2))
+            halves.append(diagonal(other, n * stations // 2, stations // 2, 0, SUB))
+        finish(previous, previous, jnp.concatenate(halves, axis=0))
+
     def pair(step, carry):
-        one_station(2 * step, 0)
-        one_station(2 * step + 1, 1)
+        one_step(2 * step, 0)
+        one_step(2 * step + 1, 1)
         return carry
 
+    grams[1] = jnp.zeros(grams.shape[1:], jnp.float32)
+    build(0, 0, range(parts))
     lax.fori_loop(0, own_count // 2, pair, 0)
+    finish(own_count - 1, own_count - 1, diagonal(1, 0, stations, 0, SUB))
     for a in range(own_count):
         order[:, a, :] = sums[a]
     square = (LAGS, LAGS)
@@ -498,8 +514,10 @@
         scratch_shapes=[
             pltpu.VMEM((2, parts, length, LANES), jnp.float32),
             pltpu.VMEM((2, parts, length - 8, LANES), jnp.float32),
+            pltpu.VMEM((2, parts * nk, LAGS), jnp.bfloat16),
             pltpu.VMEM((nk, own_count, LANES), jnp.float32),
             pltpu.VMEM((SUB, stations, parts * nk), jnp.float32),
+            pltpu.VMEM((SUB * stations, parts * nk), jnp.bfloat16),
             pltpu.VMEM((own_count * SUB // LANES, stations, LANES), jnp.float32),
             pltpu.VMEM((2, SUB * stations, LAGS), jnp.float32),
             pltpu.VMEM((own_count, rows, LAGS), jnp.float32),

time: 43.3 us -> 40.1 us (0.926)
  Pallas kernels: 41 us -> 37.7 us
    pallas_call x1, Pallas kernels: 18 us -> 14.7 us  [on_device(): pl.pallas_call(functools.partial(lag_kernel, n_sta, n_seg, slots), out_sh...]
where the time goes in v5:
time: 40.1 us; the launch traced here: 39.9 us
  Pallas kernels  37.7 us (94%)
  local copies, waits for them, and re-layouts  1.51 us (4%)
  between operations  0.65 us (2%)
    pallas_call x1, Pallas kernels, on_device(): pl.pallas_call(functools.partial(gather_kernel, n_sta, n_seg), out_shape=...  23 us
    pallas_call x1, Pallas kernels, on_device(): pl.pallas_call(functools.partial(lag_kernel, n_sta, n_seg, slots), out_sh...  14.7 us
    unnamed x4, local copies, waits for them, and re-layouts  1.51 us

profile of v5, /device:TPU:3, one launch (start us, length us, event | category | flops | bytes accessed | tf_op | source)
XLA Modules:
  0.0 39.9 jit_solution(17532260633439076770)
XLA Ops:
  0.6 0.0 copy-start
  0.6 0.8 %copy-done = bf16[16,2048]{1,0:T(8,128)(2,1)S(1)} copy-done((bf16[16,2048]{1,0:T(8,128)(2,1)S(1)}, bf16[16,2048]{1,0:T(8,128)(2,1)}, u32[]{:S(2)}) %copy-start) | copy-done | bytes 65560
  1.5 0.0 copy-start.1
  1.5 0.7 %copy-done.1 = s32[8,4]{0,1:T(4,128)S(1)} copy-done((s32[8,4]{0,1:T(4,128)S(1)}, s32[8,4]{0,1:T(4,128)}, u32[]{:S(2)}) %copy-start.1) | copy-done | bytes 152
  2.2 23.0 %whiten_and_gather.1 = (bf16[65,16,128]{2,1,0:T(8,128)(2,1)S(1)}, f32[16,80,128]{2,1,0:T(8,128)S(1)}, bf16[2,65,16,128]{3,2,1,0:T(8,128)(2,1)S(1)}) custom-call(bf16[16,2048]{1,0:T(8,128)(2,1)S(1)} %copy-done, s32[4,8]{1,0:T(4,128)S(1)} %bitcast.1), custom_call_target="tpu_custom_call" | custom-call | tf_op jit(solution)/shard_map/whiten_and_gather/pallas_call | solution.py:478
  25.2 14.7 %correlate.1 = (bf16[16,2048]{1,0:T(8,128)(2,1)}, bf16[32,16,512]{2,1,0:T(8,128)(2,1)}) custom-call(bf16[65,16,128]{2,1,0:T(8,128)(2,1)S(1)} %get-tuple-element.5.own, f32[16,80,128]{2,1,0:T(8,128)S(1)} %get-tuple-element.6.series, bf16[2,65,16,128]{3,2,1,0:T(8,128)(2,1)S(1)} %get-tuple-element.7.received), custom_call_target="tpu_custom_call" | custom-call | tf_op jit(solution)/shard_map/correlate/pallas_call | solution.py:506
Async XLA Ops:
  0.6 0.8 %copy-start = (bf16[16,2048]{1,0:T(8,128)(2,1)S(1)}, bf16[16,2048]{1,0:T(8,128)(2,1)}, u32[]{:S(2)}) copy-start(bf16[16,2048]{1,0:T(8,128)(2,1)} %records.1) | copy-start | bytes 196612
  1.5 0.7 %copy-start.1 = (s32[8,4]{0,1:T(4,128)S(1)}, s32[8,4]{0,1:T(4,128)}, u32[]{:S(2)}) copy-start(s32[8,4]{0,1:T(4,128)} %param.3) | copy-start | bytes 388

commit v6 on v5

--- a/solution.py
+++ b/solution.py
@@ -153,6 +153,7 @@
     own,
     series,
     received,
+    left,
     held,
     names,
     flat,
@@ -298,6 +299,15 @@
             along_z_up(j).wait_recv()
             send(j)
 
+    def turn(source):
+        flat[...] = received[source, : n_seg * n1].astype(jnp.float32)
+        for b in range(own_count):
+            across = flat[:, b, :].T
+            left[source, :, b, :] = jnp.concatenate(
+                [across[c * SUB : (c + 1) * SUB] for c in range(LANES // SUB)], axis=1
+            )
+
+    turn(y)
     for j in range(n_seg):
         for d in range(1, depth):
             along_y(j, d).wait()
@@ -310,8 +320,11 @@
         def _():
             along_z_down(j).wait_send()
 
-
-def lag_kernel(n_sta, n_seg, slots, own, series, received, white, out, turned, shifted, rhs, rec, left, lhs, tails, grams, sums, order):
+    for d in range(1, depth):
+        turn((y + d) % depth)
+
+
+def lag_kernel(n_sta, n_seg, slots, own, series, received, left, white, out, turned, shifted, rhs, lhs, tails, grams, sums, order):
     depth = n_sta // n_seg
     nk, own_count = own.shape[0] - 1, own.shape[1]
     stations = depth * own_count
@@ -326,14 +339,10 @@
     for t in range(n1):
         white[:, t * LANES : (t + 1) * LANES] = own[g * n1 + t]
 
-    for y in range(depth):
-        rec[...] = received[y, :nk].astype(jnp.float32)
-        for b in range(own_count):
-            across = rec[:, b, :].T
-            left[:, y * own_count + b, :] = jnp.concatenate(
-                [across[c * SUB : (c + 1) * SUB] for c in range(parts)], axis=1
-            )
-    lhs[...] = left[...].reshape(SUB * stations, parts * nk).astype(jnp.bfloat16)
+    for source in range(depth):
+        lhs[:, source * own_count : (source + 1) * own_count, :] = left[source].astype(
+            jnp.bfloat16
+        )
 
     lane = lax.broadcasted_iota(jnp.int32, (nk, LANES), 1)
     for first in range(0, own_count, per_tile):
@@ -347,7 +356,7 @@
                 piece = jnp.where(lane // SUB == q, moved, piece)
             pieces.append(piece)
         ends_of = jnp.dot(
-            lhs[...],
+            lhs[...].reshape(SUB * stations, parts * nk),
             jnp.concatenate(pieces, axis=0).astype(jnp.bfloat16),
             preferred_element_type=jnp.float32,
         )
@@ -435,7 +444,9 @@
         for n in range(2):
             columns = slice(n * LAGS // 2, (n + 1) * LAGS // 2)
             grams[half, :, columns] = jnp.dot(
-                lhs[...], rhs[half, :, columns], preferred_element_type=jnp.float32
+                lhs[...].reshape(SUB * stations, parts * nk),
+                rhs[half, :, columns],
+                preferred_element_type=jnp.float32,
             )
             build(following, other, range(n * parts // 2, (n + 1) * parts // 2))
             halves.append(diagonal(other, n * stations // 2, stations // 2, 0, SUB))
@@ -475,15 +486,16 @@
     blocks = own_count // BS
     slots = max(2, 2 * blocks * DESTS // n_sta)
     vmem = pl.BlockSpec(memory_space=pltpu.VMEM)
-    own, series, received = pl.pallas_call(
+    own, series, received, left = pl.pallas_call(
         functools.partial(gather_kernel, n_sta, n_seg),
         out_shape=(
             jax.ShapeDtypeStruct((nk + 1, own_count, LANES), jnp.bfloat16),
             jax.ShapeDtypeStruct((own_count, length, LANES), jnp.float32),
             jax.ShapeDtypeStruct((depth, nk + 1, own_count, LANES), jnp.bfloat16),
+            jax.ShapeDtypeStruct((depth, SUB, own_count, LANES // SUB * nk), jnp.float32),
         ),
         in_specs=[vmem] * 2,
-        out_specs=(vmem,) * 3,
+        out_specs=(vmem,) * 4,
         scratch_shapes=[
             pltpu.VMEM((n_seg, own_count, seg_len), jnp.bfloat16),
             pltpu.VMEM((own_count, LANES), jnp.float32),
@@ -509,15 +521,13 @@
             jax.ShapeDtypeStruct((own_count, seg_len), jnp.bfloat16),
             jax.ShapeDtypeStruct((rows, own_count, LAGS), jnp.bfloat16),
         ),
-        in_specs=[vmem] * 3,
+        in_specs=[vmem] * 4,
         out_specs=(vmem,) * 2,
         scratch_shapes=[
             pltpu.VMEM((2, parts, length, LANES), jnp.float32),
             pltpu.VMEM((2, parts, length - 8, LANES), jnp.float32),
             pltpu.VMEM((2, parts * nk, LAGS), jnp.bfloat16),
-            pltpu.VMEM((nk, own_count, LANES), jnp.float32),
-            pltpu.VMEM((SUB, stations, parts * nk), jnp.float32),
-            pltpu.VMEM((SUB * stations, parts * nk), jnp.bfloat16),
+            pltpu.VMEM((SUB, stations, parts * nk), jnp.bfloat16),
             pltpu.VMEM((own_count * SUB // LANES, stations, LANES), jnp.float32),
             pltpu.VMEM((2, SUB * stations, LAGS), jnp.float32),
             pltpu.VMEM((own_count, rows, LAGS), jnp.float32),
@@ -525,7 +535,7 @@
         ],
         compiler_params=pltpu.CompilerParams(vmem_limit_bytes=48 * 2**20),
         name="correlate",
-    )(own, series, received)
+    )(own, series, received, left)
     return white, correlations
 
 

time: 40.1 us -> 39.5 us (0.985)
  Pallas kernels: 37.7 us -> 37.2 us
    pallas_call x1, Pallas kernels: 14.7 us -> 13.5 us  [on_device(): pl.pallas_call(functools.partial(lag_kernel, n_sta, n_seg, slots), out_sh...]
    pallas_call x1, Pallas kernels: 23 us -> 23.6 us  [on_device(): pl.pallas_call(functools.partial(gather_kernel, n_sta, n_seg), out_shape=...]
where the time goes in v6:
time: 39.5 us; the launch traced here: 39.3 us
  Pallas kernels  37.2 us (94%)
  local copies, waits for them, and re-layouts  1.51 us (4%)
  between operations  0.65 us (2%)
    pallas_call x1, Pallas kernels, on_device(): pl.pallas_call(functools.partial(gather_kernel, n_sta, n_seg), out_shape=...  23.6 us
    pallas_call x1, Pallas kernels, on_device(): pl.pallas_call(functools.partial(lag_kernel, n_sta, n_seg, slots), out_sh...  13.5 us
    unnamed x4, local copies, waits for them, and re-layouts  1.51 us

profile of v6, /device:TPU:3, one launch (start us, length us, event | category | flops | bytes accessed | tf_op | source)
XLA Modules:
  0.0 39.3 jit_solution(8655144670283781763)
XLA Ops:
  0.6 0.0 copy-start
  0.6 0.8 %copy-done = bf16[16,2048]{1,0:T(8,128)(2,1)S(1)} copy-done((bf16[16,2048]{1,0:T(8,128)(2,1)S(1)}, bf16[16,2048]{1,0:T(8,128)(2,1)}, u32[]{:S(2)}) %copy-start) | copy-done | bytes 65560
  1.5 0.0 copy-start.1
  1.5 0.7 %copy-done.1 = s32[8,4]{0,1:T(4,128)S(1)} copy-done((s32[8,4]{0,1:T(4,128)S(1)}, s32[8,4]{0,1:T(4,128)}, u32[]{:S(2)}) %copy-start.1) | copy-done | bytes 152
  2.2 23.6 %whiten_and_gather.1 = (bf16[65,16,128]{2,1,0:T(8,128)(2,1)S(1)}, f32[16,80,128]{2,1,0:T(8,128)S(1)}, bf16[2,65,16,128]{3,2,1,0:T(8,128)(2,1)S(1)}, f32[2,16,16,512]{3,2,1,0:T(8,128)S(1)}) custom-call(bf16[16,2048]{1,0:T(8,128)(2,1)S(1)} %copy-done, s32[4,8]{1,0:T(4,128)S(1)} %bitcast.1), custom_call_target="tpu_custom_call" | custom-call | tf_op jit(solution)/shard_map/whiten_and_gather/pallas_call | solution.py:489
  25.8 13.5 %correlate.1 = (bf16[16,2048]{1,0:T(8,128)(2,1)}, bf16[32,16,512]{2,1,0:T(8,128)(2,1)}) custom-call(bf16[65,16,128]{2,1,0:T(8,128)(2,1)S(1)} %get-tuple-element.6.own, f32[16,80,128]{2,1,0:T(8,128)S(1)} %get-tuple-element.7.series, bf16[2,65,16,128]{3,2,1,0:T(8,128)(2,1)S(1)} %get-tuple-element.8.received, f32[2,16,16,512]{3,2,1,0:T(8,128)S(1)} %get-tuple-element.9.left), custom_call_target="tpu_custom_call" | custom-call | tf_op jit(solution)/shard_map/correlate/pallas_call | solution.py:518
Async XLA Ops:
  0.6 0.8 %copy-start = (bf16[16,2048]{1,0:T(8,128)(2,1)S(1)}, bf16[16,2048]{1,0:T(8,128)(2,1)}, u32[]{:S(2)}) copy-start(bf16[16,2048]{1,0:T(8,128)(2,1)} %records.1) | copy-start | bytes 196612
  1.5 0.7 %copy-start.1 = (s32[8,4]{0,1:T(4,128)S(1)}, s32[8,4]{0,1:T(4,128)}, u32[]{:S(2)}) copy-start(s32[8,4]{0,1:T(4,128)} %param.3) | copy-start | bytes 388

commit v7 on v6

--- a/solution.py
+++ b/solution.py
@@ -452,14 +452,14 @@
             halves.append(diagonal(other, n * stations // 2, stations // 2, 0, SUB))
         finish(previous, previous, jnp.concatenate(halves, axis=0))
 
-    def pair(step, carry):
-        one_step(2 * step, 0)
-        one_step(2 * step + 1, 1)
+    def four(step, carry):
+        for k in range(4):
+            one_step(4 * step + k, k % 2)
         return carry
 
     grams[1] = jnp.zeros(grams.shape[1:], jnp.float32)
     build(0, 0, range(parts))
-    lax.fori_loop(0, own_count // 2, pair, 0)
+    lax.fori_loop(0, own_count // 4, four, 0)
     finish(own_count - 1, own_count - 1, diagonal(1, 0, stations, 0, SUB))
     for a in range(own_count):
         order[:, a, :] = sums[a]

time: 39.5 us -> 39.9 us (1.010)
  no operation moved by 1% of the time
where the time goes in v7:
time: 39.9 us; the launch traced here: 39.7 us
  Pallas kernels  37.5 us (94%)
  local copies, waits for them, and re-layouts  1.51 us (4%)
  between operations  0.65 us (2%)
    pallas_call x1, Pallas kernels, on_device(): pl.pallas_call(functools.partial(gather_kernel, n_sta, n_seg), out_shape=...  23.6 us
    pallas_call x1, Pallas kernels, on_device(): pl.pallas_call(functools.partial(lag_kernel, n_sta, n_seg, slots), out_sh...  13.9 us
    unnamed x4, local copies, waits for them, and re-layouts  1.51 us

profile of v7, /device:TPU:3, one launch (start us, length us, event | category | flops | bytes accessed | tf_op | source)
XLA Modules:
  0.0 39.7 jit_solution(4833097419966382023)
XLA Ops:
  0.6 0.0 copy-start
  0.6 0.8 %copy-done = bf16[16,2048]{1,0:T(8,128)(2,1)S(1)} copy-done((bf16[16,2048]{1,0:T(8,128)(2,1)S(1)}, bf16[16,2048]{1,0:T(8,128)(2,1)}, u32[]{:S(2)}) %copy-start) | copy-done | bytes 65560
  1.5 0.0 copy-start.1
  1.5 0.7 %copy-done.1 = s32[8,4]{0,1:T(4,128)S(1)} copy-done((s32[8,4]{0,1:T(4,128)S(1)}, s32[8,4]{0,1:T(4,128)}, u32[]{:S(2)}) %copy-start.1) | copy-done | bytes 152
  2.2 23.6 %whiten_and_gather.1 = (bf16[65,16,128]{2,1,0:T(8,128)(2,1)S(1)}, f32[16,80,128]{2,1,0:T(8,128)S(1)}, bf16[2,65,16,128]{3,2,1,0:T(8,128)(2,1)S(1)}, f32[2,16,16,512]{3,2,1,0:T(8,128)S(1)}) custom-call(bf16[16,2048]{1,0:T(8,128)(2,1)S(1)} %copy-done, s32[4,8]{1,0:T(4,128)S(1)} %bitcast.1), custom_call_target="tpu_custom_call" | custom-call | tf_op jit(solution)/shard_map/whiten_and_gather/pallas_call | solution.py:489
  25.8 13.9 %correlate.1 = (bf16[16,2048]{1,0:T(8,128)(2,1)}, bf16[32,16,512]{2,1,0:T(8,128)(2,1)}) custom-call(bf16[65,16,128]{2,1,0:T(8,128)(2,1)S(1)} %get-tuple-element.6.own, f32[16,80,128]{2,1,0:T(8,128)S(1)} %get-tuple-element.7.series, bf16[2,65,16,128]{3,2,1,0:T(8,128)(2,1)S(1)} %get-tuple-element.8.received, f32[2,16,16,512]{3,2,1,0:T(8,128)S(1)} %get-tuple-element.9.left), custom_call_target="tpu_custom_call" | custom-call | tf_op jit(solution)/shard_map/correlate/pallas_call | solution.py:518
Async XLA Ops:
  0.6 0.8 %copy-start = (bf16[16,2048]{1,0:T(8,128)(2,1)S(1)}, bf16[16,2048]{1,0:T(8,128)(2,1)}, u32[]{:S(2)}) copy-start(bf16[16,2048]{1,0:T(8,128)(2,1)} %records.1) | copy-start | bytes 196612
  1.5 0.7 %copy-start.1 = (s32[8,4]{0,1:T(4,128)S(1)}, s32[8,4]{0,1:T(4,128)}, u32[]{:S(2)}) copy-start(s32[8,4]{0,1:T(4,128)} %param.3) | copy-start | bytes 388
